TPU v7x, 32 devices: a whole 2x2x4 slice. The times are simulated.
32 devices in a mesh: grp: 4 (over y, x), seq: 8 (over z, core).
Axes of the slice: x: 2, y: 2, z: 4, core: 2. Of those that a mesh axis runs over, the one named last changes fastest.
Arguments:
- thinker_input: bfloat16 [4, 32, 3584], P(None, 'grp'), as said below
- thinker_gain: float32 [3584], replicated, may hold values from 0.25 to 1.75
- thinker_qkv: bfloat16 [3584, 4608], P('seq'), may hold values from -0.09375 to 0.09375
- thinker_out: bfloat16 [3584, 3584], P('seq'), may hold values from -0.09375 to 0.09375
- talker_proj: bfloat16 [3584, 896], P('seq'), may hold values from -0.09375 to 0.09375
- code_table: bfloat16 [8448, 896], P('seq'), may hold values from -6 to 6
- talker_gain: float32 [896], replicated, may hold values from 0.25 to 1.75
- talker_qkv: bfloat16 [896, 2560], replicated, may hold values from -0.1875 to 0.1875
- talker_out: bfloat16 [1536, 896], replicated, may hold values from -0.15625 to 0.15625
- text_keys: bfloat16 [32, 1024, 512], P('grp', 'seq'), as said below
- text_values: bfloat16 [32, 1024, 512], P('grp', 'seq'), may hold values from -72 to 72
- audio_keys: bfloat16 [32, 1024, 512], P('grp', 'seq'), as said below
- audio_values: bfloat16 [32, 1024, 512], P('grp', 'seq'), may hold values from -72 to 72
- text_len: int32 [32], P('grp'), may hold values from 2 to 1024
- audio_len: int32 [32], P('grp'), may hold values from 2 to 1024
- text_pos: int32 [32, 4], P('grp'), may hold values from 0 to 1027
- audio_pos: int32 [32, 4], P('grp'), may hold values from 0 to 1027
- code_ids: int32 [32, 4], P('grp'), may hold values from 0 to 8447
Outputs:
- thinker_hidden: bfloat16 [4, 32, 3584], P(None, 'grp')
- talker_hidden: bfloat16 [4, 32, 896], P(None, 'grp', 'seq')
Inputs may be any that keep to these rules, and one draw needn't show every extreme that they name: Cache positions 0 .. text_len - 1 of a conversation are live. Cache positions 0 .. audio_len - 1 of a conversation are live. `thinker_input`: real-valued, of order one per feature. `text_keys`: real-valued. `audio_keys`: real-valued.
All inputs are finite; a program needn't handle non-finite values.
Results may differ from a plain program's by a relative error of at most 0.028.
Values may be sent and summed in bfloat16 or wider, within the bound.
A program may use at most 128 MiB of HBM per device.

v0:
```python
import jax
import jax.numpy as jnp
from jax import lax
from jax.sharding import PartitionSpec as P

D = 3584
HQ = 28
HK = 4
HD = 128
TD = 896
AHQ = 12
AHK = 4
AHD = 128


EPSILON = 1e-06
THETA = 1000000.0
NEGATIVE = -1e30


def rotate(vectors, positions):
    width = vectors.shape[-1]
    half = width // 2
    freqs = jnp.exp(
        jnp.arange(half).astype(jnp.float32) * (-2.0 * jnp.log(jnp.float32(THETA)) / width)
    )
    angles = positions.astype(jnp.float32)[:, None] * freqs[None, :]
    cosine = jnp.cos(angles)[:, None, :]
    sine = jnp.sin(angles)[:, None, :]
    first = vectors[..., :half]
    second = vectors[..., half:]
    return jnp.concatenate(
        [first * cosine - second * sine, second * cosine + first * sine], axis=-1
    )


def attend(query, keys, values, new_keys, new_values, live, fresh_live):
    batch, heads, group, width = query.shape
    count = keys.shape[1]
    scale = width ** (-0.5)
    key_four = keys.reshape(batch, count, heads, width)
    value_four = values.reshape(batch, count, heads, width)
    cached = (
        jnp.einsum("bkgd,btkd->bkgt", query, key_four, preferred_element_type=jnp.float32) * scale
    )
    fresh = (
        jnp.einsum("bkgd,bskd->bkgs", query, new_keys, preferred_element_type=jnp.float32) * scale
    )
    live_mask = live[:, None, None, :]
    fresh_mask = fresh_live[None, None, None, :]
    cached = jnp.where(live_mask, cached, NEGATIVE)
    fresh = jnp.where(fresh_mask, fresh, NEGATIVE)
    local_peak = jnp.maximum(cached.max(-1), fresh.max(-1))
    flat_width = heads * group * width
    peak = lax.pmax(local_peak, "seq")
    weight_cached = jnp.where(live_mask, jnp.exp(cached - peak[..., None]), 0.0)
    weight_fresh = jnp.where(fresh_mask, jnp.exp(fresh - peak[..., None]), 0.0)
    total = weight_cached.sum(-1) + weight_fresh.sum(-1)
    summed = jnp.einsum(
        "bkgt,btkd->bkgd",
        weight_cached.astype(jnp.bfloat16),
        value_four,
        preferred_element_type=jnp.float32,
    )
    summed = summed + jnp.einsum(
        "bkgs,bskd->bkgd",
        weight_fresh.astype(jnp.bfloat16),
        new_values,
        preferred_element_type=jnp.float32,
    )
    total, summed = (total, summed)
    total, summed = lax.psum((total, summed), "seq")
    return (summed / total[..., None]).reshape(batch, flat_width).astype(jnp.bfloat16)


def body(
    thinker_input,
    thinker_gain,
    thinker_qkv,
    thinker_out,
    talker_proj,
    code_table,
    talker_gain,
    talker_qkv,
    talker_out,
    text_keys,
    text_values,
    audio_keys,
    audio_values,
    text_len,
    audio_len,
    text_pos,
    audio_pos,
    code_ids,
):
    steps = thinker_input.shape[0]
    batch = thinker_input.shape[1]
    index = lax.axis_index("seq")
    shards = lax.axis_size("seq")
    text_kv = HK * HD
    audio_q = AHQ * AHD
    audio_kv = AHK * AHD
    text_count = text_keys.shape[1]
    audio_count = audio_keys.shape[1]
    text_live = (index * text_count + jnp.arange(text_count))[None, :] < text_len[:, None]
    audio_live = (index * audio_count + jnp.arange(audio_count))[None, :] < audio_len[:, None]
    table_rows = code_table.shape[0]
    table_ids = index * table_rows + jnp.arange(table_rows)
    feature_rows = thinker_qkv.shape[0]
    output_rows = thinker_out.shape[0]
    bridge_rows = talker_proj.shape[0]
    talker_cols = talker_out.shape[1] // shards
    out_slice = lax.dynamic_slice_in_dim(talker_out, index * talker_cols, talker_cols, 1)
    new_text_keys = jnp.zeros((batch, steps, HK, HD), jnp.bfloat16)
    new_text_values = jnp.zeros((batch, steps, HK, HD), jnp.bfloat16)
    new_audio_keys = jnp.zeros((batch, steps, AHK, AHD), jnp.bfloat16)
    new_audio_values = jnp.zeros((batch, steps, AHK, AHD), jnp.bfloat16)
    thinker_list = []
    talker_list = []
    for step in range(steps):
        fresh_live = (jnp.arange(steps) <= step) & (index == 0)
        inputs = thinker_input[step].astype(jnp.float32)
        scaled = (inputs * thinker_gain).astype(jnp.bfloat16)
        mine_scaled = lax.dynamic_slice_in_dim(scaled, index * feature_rows, feature_rows, 1)
        partial_value = jnp.dot(mine_scaled, thinker_qkv, preferred_element_type=jnp.float32)
        squares = jnp.sum(inputs * inputs, axis=-1)
        projected = lax.psum(partial_value, "seq")
        projected = projected * lax.rsqrt(squares / D + EPSILON)[:, None]
        query = rotate(projected[:, :D].reshape(batch, HQ, HD), text_pos[:, step]).astype(
            jnp.bfloat16
        )
        key = rotate(
            projected[:, D : D + text_kv].reshape(batch, HK, HD), text_pos[:, step]
        ).astype(jnp.bfloat16)
        value = projected[:, D + text_kv :].reshape(batch, HK, HD).astype(jnp.bfloat16)
        new_text_keys = new_text_keys.at[:, step].set(key)
        new_text_values = new_text_values.at[:, step].set(value)
        attended = attend(
            query.reshape(batch, HK, HQ // HK, HD),
            text_keys,
            text_values,
            new_text_keys,
            new_text_values,
            text_live,
            fresh_live,
        )
        mine_attended = lax.dynamic_slice_in_dim(attended, index * output_rows, output_rows, 1)
        contribution = lax.psum(
            jnp.dot(mine_attended, thinker_out, preferred_element_type=jnp.float32), "seq"
        )
        hidden = (inputs + contribution).astype(jnp.bfloat16)
        thinker_list.append(hidden)
        picked = (code_ids[:, step][:, None] == table_ids[None, :]).astype(jnp.bfloat16)
        mine_hidden = lax.dynamic_slice_in_dim(hidden, index * bridge_rows, bridge_rows, 1)
        pieces = jnp.dot(mine_hidden, talker_proj, preferred_element_type=jnp.float32) + jnp.dot(
            picked, code_table, preferred_element_type=jnp.float32
        )
        talker_in = lax.psum(pieces, "seq")
        normed = (
            talker_in
            * lax.rsqrt(jnp.sum(talker_in * talker_in, axis=-1, keepdims=True) / TD + EPSILON)
            * talker_gain
        ).astype(jnp.bfloat16)
        spoken = jnp.dot(normed, talker_qkv, preferred_element_type=jnp.float32)
        audio_query = rotate(
            spoken[:, :audio_q].reshape(batch, AHQ, AHD), audio_pos[:, step]
        ).astype(jnp.bfloat16)
        audio_key = rotate(
            spoken[:, audio_q : audio_q + audio_kv].reshape(batch, AHK, AHD), audio_pos[:, step]
        ).astype(jnp.bfloat16)
        audio_value = spoken[:, audio_q + audio_kv :].reshape(batch, AHK, AHD).astype(jnp.bfloat16)
        new_audio_keys = new_audio_keys.at[:, step].set(audio_key)
        new_audio_values = new_audio_values.at[:, step].set(audio_value)
        heard = attend(
            audio_query.reshape(batch, AHK, AHQ // AHK, AHD),
            audio_keys,
            audio_values,
            new_audio_keys,
            new_audio_values,
            audio_live,
            fresh_live,
        )
        residual = lax.dynamic_slice_in_dim(talker_in, index * talker_cols, talker_cols, 1)
        talker_list.append(
            (residual + jnp.dot(heard, out_slice, preferred_element_type=jnp.float32)).astype(
                jnp.bfloat16
            )
        )
    return (jnp.stack(thinker_list), jnp.stack(talker_list))


def solution(mesh):
    return jax.shard_map(
        body,
        mesh=mesh,
        in_specs=(
            P(None, "grp", None),
            P(),
            P("seq", None),
            P("seq", None),
            P("seq", None),
            P("seq", None),
            P(),
            P(),
            P(),
            P("grp", "seq", None),
            P("grp", "seq", None),
            P("grp", "seq", None),
            P("grp", "seq", None),
            P("grp"),
            P("grp"),
            P("grp", None),
            P("grp", None),
            P("grp", None),
        ),
        out_specs=(P(None, "grp", None), P(None, "grp", "seq")),
        check_vma=False,
    )
```

profile of v0, /device:TPU:0, one launch (start us, length us, event | category | flops | bytes accessed | tf_op | source)
XLA Modules:
  0.0 534.7 jit_solution(11168622472816012938)
XLA Ops:
  9.9 3.8 fusion.223
  22.2 55.4 %all-reduce.26.cloned.1.call-done = (f32[8,4608]{1,0:T(8,128)}, f32[8,4608]{1,0:T(8,128)}, f32[8,4608]{1,0:T(8,128)}, f32[8,4608]{1,0:T(8,128)}) async-done(((f32[8,4608]{1,0:T(8,128)}, f32[8,4608]{1,0:T(8,128)}, f32[8,4608]{1,0:T(8,128)}, f32[8,4608]{1,0:T(8,128)}), (f32[8,4608]{1,0:T(8,128)}, f32[8,4608]{1,0:T(8,128)}, f32[8,4608]{1,0:T(8,128)}, f32[8,4608]{1,0:T(8,128)})) %all-reduce.26.cloned.1.call-update) | async-done | bytes 589840 | tf_op jit(solution)/shard_map/psum | solution.py:127
  95.7 2.6 fusion.302
  99.0 2.6 fusion.300
  104.7 2.7 fusion.298
  111.1 2.7 fusion.296
  116.1 26.9 %all-reduce.11 = (f32[8,4,7]{2,1,0:T(4,128)S(1)}, f32[8,4,7]{2,1,0:T(4,128)S(1)}, f32[8,4,7]{2,1,0:T(4,128)S(1)}, f32[8,4,7]{2,1,0:T(4,128)S(1)}) all-reduce(f32[8,4,7]{2,1,0:T(4,128)} %max.43, f32[8,4,7]{2,1,0:T(4,128)} %max.42, f32[8,4,7]{2,1,0:T(4,128)} %max.41, f32[8,4,7]{2,1,0:T(4,128)} %max.40), channel_id=1, replica_groups=mesh['grp'=4,'seq'=8] {'seq'}, use_global_device_ids=true, to_apply=%region_34.35 | all-reduce | flops 896 | bytes 7168 | tf_op jit(solution)/shard_map/pmax | solution.py:55
  151.2 2.4 convolution_add_fusion.2
  153.6 2.4 convolution_add_fusion.3
  160.1 2.4 convolution_add_fusion
  167.4 26.8 %all-reduce.6 = (f32[8,4,7]{2,1,0:T(4,128)}, f32[8,4,7]{2,1,0:T(4,128)S(1)}, f32[8,4,7]{2,1,0:T(4,128)S(1)}, f32[8,4,7]{2,1,0:T(4,128)S(1)}) all-reduce(f32[8,4,7]{2,1,0:T(4,128)S(1)} %add.356, f32[8,4,7]{2,1,0:T(4,128)S(1)} %add.350, f32[8,4,7]{2,1,0:T(4,128)S(1)} %add.344, ...), channel_id=1, replica_groups=mesh['grp'=4,'seq'=8] {'seq'}, use_global_device_ids=true, to_apply=%region_38.39 | all-reduce | flops 896 | bytes 7168 | tf_op jit(solution)/shard_map/psum | solution.py:72
  194.2 24.7 %all-reduce.24.cloned.1.call-done = (f32[8,4,7,128]{3,2,1,0:T(8,128)}, f32[8,4,7,128]{3,2,1,0:T(8,128)}, f32[8,4,7,128]{3,2,1,0:T(8,128)}, f32[8,4,7,128]{3,2,1,0:T(8,128)}) async-done(((f32[8,4,7,128]{3,2,1,0:T(8,128)}, f32[8,4,7,128]{3,2,1,0:T(8,128)}, f32[8,4,7,128]{3,2,1,0:T(8,128)}, f32[8,4,7,128]{3,2,1,0:T(8,128)}), (f32[8,4,7,128]{3,2,1,0:T(8,128)}, f32[8,4,7,128]{3,2,1,0:T(8,128)}, ...) | async-done | bytes 458768 | tf_op jit(solution)/shard_map/psum | solution.py:72
  234.8 54.1 %all-reduce.22.cloned.1.call-done = (f32[8,3584]{1,0:T(8,128)}, f32[8,3584]{1,0:T(8,128)}, f32[8,3584]{1,0:T(8,128)}, f32[8,3584]{1,0:T(8,128)}) async-done(((f32[8,3584]{1,0:T(8,128)}, f32[8,3584]{1,0:T(8,128)}, f32[8,3584]{1,0:T(8,128)}, f32[8,3584]{1,0:T(8,128)}), (f32[8,3584]{1,0:T(8,128)}, f32[8,3584]{1,0:T(8,128)}, f32[8,3584]{1,0:T(8,128)}, f32[8,3584]{1,0:T(8,128)})) %all-reduce.22.cloned.1.call-update) | async-done | bytes 458768 | tf_op jit(solution)/shard_map/psum | solution.py:148
  298.9 51.4 %all-reduce.20.cloned.1.call-done = (f32[8,896]{1,0:T(8,128)}, f32[8,896]{1,0:T(8,128)}, f32[8,896]{1,0:T(8,128)}, f32[8,896]{1,0:T(8,128)}) async-done(((f32[8,896]{1,0:T(8,128)}, f32[8,896]{1,0:T(8,128)}, f32[8,896]{1,0:T(8,128)}, f32[8,896]{1,0:T(8,128)}), (f32[8,896]{1,0:T(8,128)}, f32[8,896]{1,0:T(8,128)}, f32[8,896]{1,0:T(8,128)}, f32[8,896]{1,0:T(8,128)})) %all-reduce.20.cloned.1.call-update) | async-done | bytes 114704 | tf_op jit(solution)/shard_map/psum | solution.py:158
  351.2 3.2 fusion.188
  355.1 3.1 fusion.187
  359.0 3.0 fusion.186
  372.6 3.2 fusion.306
  375.8 3.2 fusion.308
  382.8 3.2 fusion.310
  388.3 2.6 fusion.304
  396.2 29.2 %all-reduce.10 = (f32[8,4,3]{2,1,0:T(4,128)S(1)}, f32[8,4,3]{2,1,0:T(4,128)}, f32[8,4,3]{2,1,0:T(4,128)}, f32[8,4,3]{2,1,0:T(4,128)S(1)}) all-reduce(f32[8,4,3]{2,1,0:T(4,128)S(1)} %max.47, f32[8,4,3]{2,1,0:T(4,128)S(1)} %max.44, f32[8,4,3]{2,1,0:T(4,128)S(1)} %max.45, f32[8,4,3]{2,1,0:T(4,128)S(1)} %max.46), channel_id=1, replica_groups=mesh['grp'=4,'seq'=8] {'seq'}, use_global_device_ids=true, to_apply=%region_71.72 | all-reduce | flops 384 | bytes 3072 | tf_op jit(solution)/shard_map/pmax | solution.py:55
  425.5 2.4 fusion.24
  464.0 53.8 %all-reduce.18.cloned.1.call-done = (f32[8,4,3,128]{3,2,1,0:T(4,128)}, f32[8,4,3]{2,1,0:T(4,128)}, f32[8,4,3,128]{3,2,1,0:T(4,128)}, f32[8,4,3]{2,1,0:T(4,128)},...) async-done(((f32[8,4,3,128]{3,2,1,0:T(4,128)}, f32[8,4,3]{2,1,0:T(4,128)}, f32[8,4,3,128]{3,2,1,0:T(4,128)}, ...) | async-done | bytes 198160 | tf_op jit(solution)/shard_map/psum | solution.py:72
  (368 shorter events, 152.1 us)
Async XLA Ops:
  7.2 218.7 %copy-start = (bf16[448,3584]{1,0:T(8,128)(2,1)S(1)}, bf16[448,3584]{1,0:T(8,128)(2,1)}, u32[]{:S(2)}) copy-start(bf16[448,3584]{1,0:T(8,128)(2,1)} %param.53) | copy-start | bytes 9633796
  7.2 70.4 %all-reduce.26.cloned.1.call-start = ((), (), s32[]{:S(2)}) async-start(), calls=%async_computation.4 | async-start | bytes 1179648 | tf_op jit(solution)/shard_map/psum | solution.py:127
  17.7 201.2 %all-reduce.24.cloned.1.call-start = ((), (), s32[]{:S(2)}) async-start(), calls=%async_computation.3 | async-start | bytes 1048576 | tf_op jit(solution)/shard_map/psum | solution.py:72
  77.5 10.0 %copy-start.39 = (f32[8,64]{1,0:T(8,128)S(1)}, f32[8,64]{1,0:T(8,128)}, u32[]{:S(2)}) copy-start(f32[8,64]{1,0:T(8,128)} %get-tuple-element.312) | copy-start | bytes 6148
  77.6 10.0 %copy-start.40 = (f32[8,64]{1,0:T(8,128)S(1)}, f32[8,64]{1,0:T(8,128)}, u32[]{:S(2)}) copy-start(f32[8,64]{1,0:T(8,128)} %get-tuple-element.313) | copy-start | bytes 6148
  93.9 9.2 %copy-start.24 = (bf16[8,1,4,64]{3,1,2,0:T(2,128)(2,1)S(1)}, bf16[8,1,4,64]{3,1,2,0:T(2,128)(2,1)}, u32[]{:S(2)}) copy-start(bf16[8,1,4,64]{3,1,2,0:T(2,128)(2,1)} %copy.143) | copy-start | bytes 12292
  93.9 9.2 %copy-start.25 = (bf16[8,1,4,64]{3,1,2,0:T(2,128)(2,1)S(1)}, bf16[8,1,4,64]{3,1,2,0:T(2,128)(2,1)}, u32[]{:S(2)}) copy-start(bf16[8,1,4,64]{3,1,2,0:T(2,128)(2,1)} %copy.144) | copy-start | bytes 12292
  147.2 9.9 %copy-start.3 = (bf16[8,128,512]{2,1,0:T(8,128)(2,1)S(1)}, bf16[8,128,512]{2,1,0:T(8,128)(2,1)}, u32[]{:S(2)}) copy-start(bf16[8,128,512]{2,1,0:T(8,128)(2,1)} %param.60) | copy-start | bytes 3145732
  153.6 10.5 %copy-start.63 = (pred[4]{0:T(512)(128)(4,1)S(1)}, pred[4]{0:T(512)(128)(4,1)}, u32[]{:S(2)}) copy-start(pred[4]{0:T(512)(128)(4,1)} %get-tuple-element.369) | copy-start | bytes 16
  153.6 12.2 %copy-start.62 = (pred[4]{0:T(512)(128)(4,1)S(1)}, pred[4]{0:T(512)(128)(4,1)}, u32[]{:S(2)}) copy-start(pred[4]{0:T(512)(128)(4,1)} %get-tuple-element.368) | copy-start | bytes 16
  164.0 124.9 %all-reduce.22.cloned.1.call-start = ((), (), s32[]{:S(2)}) async-start(), calls=%async_computation.2 | async-start | bytes 917504 | tf_op jit(solution)/shard_map/psum | solution.py:148
  233.5 116.7 %all-reduce.20.cloned.1.call-start = ((), (), s32[]{:S(2)}) async-start(), calls=%async_computation.1 | async-start | bytes 229376 | tf_op jit(solution)/shard_map/psum | solution.py:158
  295.8 55.4 %copy-start.21 = (f32[896]{0:T(1024)S(1)}, f32[896]{0:T(1024)}, u32[]{:S(2)}) copy-start(f32[896]{0:T(1024)} %param.56) | copy-start | bytes 10756
  298.8 219.0 %all-reduce.18.cloned.1.call-start = ((), (), s32[]{:S(2)}) async-start(), calls=%async_computation | async-start | bytes 655360 | tf_op jit(solution)/shard_map/psum | solution.py:72
  351.1 11.7 %slice-start = ((s8[4587520]{0:T(1024)(128)(4,1)}), s8[4194304]{0:T(1024)(128)(4,1)S(1)}, s32[]{:S(2)}) async-start(s8[4587520]{0:T(1024)(128)(4,1)} %bitcast.292), calls=%async_computation.5 | async-start | bytes 8388608
  369.4 22.9 %copy-start.60 = (pred[4]{0:T(512)(128)(4,1)S(1)}, pred[4]{0:T(512)(128)(4,1)}, u32[]{:S(2)}) copy-start(pred[4]{0:T(512)(128)(4,1)} %get-tuple-element.366) | copy-start | bytes 16
  372.6 13.3 %copy-start.53 = (bf16[8,4,3,64]{3,2,1,0:T(4,128)(2,1)S(1)}, bf16[8,4,3,64]{3,2,1,0:T(4,128)(2,1)}, u32[]{:S(2)}) copy-start(bf16[8,4,3,64]{3,2,1,0:T(4,128)(2,1)} %copy.169) | copy-start | bytes 36868
  381.2 12.7 %copy-start.57 = (f32[8,4,3]{2,1,0:T(4,128)S(1)}, f32[8,4,3]{2,1,0:T(4,128)}, u32[]{:S(2)}) copy-start(f32[8,4,3]{2,1,0:T(4,128)} %get-tuple-element.348) | copy-start | bytes 1156
  381.3 13.4 %copy-start.58 = (f32[8,4,3]{2,1,0:T(4,128)S(1)}, f32[8,4,3]{2,1,0:T(4,128)}, u32[]{:S(2)}) copy-start(f32[8,4,3]{2,1,0:T(4,128)} %get-tuple-element.350) | copy-start | bytes 1156
  390.9 44.6 %copy-start.54 = (bf16[8,1,4,128]{3,0,2,1:T(8,128)(2,1)S(1)}, bf16[8,1,4,128]{3,0,2,1:T(8,128)(2,1)}, u32[]{:S(2)}) copy-start(bf16[8,1,4,128]{3,0,2,1:T(8,128)(2,1)} %fusion.228) | copy-start | bytes 24580
  425.5 14.7 %copy-start.26 = (f32[8,4,3,4]{3,2,1,0:T(4,128)S(1)}, f32[8,4,3,4]{3,2,1,0:T(4,128)}, u32[]{:S(2)}) copy-start(f32[8,4,3,4]{3,2,1,0:T(4,128)} %get-tuple-element.345) | copy-start | bytes 4612
  430.3 14.7 %copy-start.29 = (f32[8,4,3]{2,1,0:T(4,128)S(1)}, f32[8,4,3]{2,1,0:T(4,128)}, u32[]{:S(2)}) copy-start(f32[8,4,3]{2,1,0:T(4,128)} %copy-done.28) | copy-start | bytes 1156
  430.3 33.0 %copy-start.11 = (bf16[8,3584]{1,0:T(8,128)(2,1)S(1)}, bf16[8,3584]{1,0:T(8,128)(2,1)}, u32[]{:S(2)}) copy-start(bf16[8,3584]{1,0:T(8,128)(2,1)} %copy-done.10) | copy-start | bytes 172036
  430.3 33.0 %copy-start.13 = (bf16[8,3584]{1,0:T(8,128)(2,1)S(1)}, bf16[8,3584]{1,0:T(8,128)(2,1)}, u32[]{:S(2)}) copy-start(bf16[8,3584]{1,0:T(8,128)(2,1)} %copy-done.12) | copy-start | bytes 172036
  (53 other events, 333.5 us)
Sparse Core Ops, SparseCore 0:
  17.8 59.6 all-reduce.25
  164.1 54.7 all-reduce.23
  233.7 55.1 all-reduce.21
  298.9 51.2 all-reduce.19
  463.4 54.4 all-reduce.17
where the time goes:
time: 539 us; the launch traced here: 535 us
  waiting for transfers between devices  239 us (44%)
  matrix products  106 us (20%)
  blocking collectives  82.9 us (15%)
  other arithmetic  51.8 us (10%)
  local copies, waits for them, and re-layouts  39.6 us (7%)
  between operations  14.9 us (3%)
    psum x2, waiting for transfers between devices, attend(): total, summed = lax.psum((total, summed), 'seq')  78.6 us
    pmax x2, blocking collectives, attend(): peak = lax.pmax(local_peak, 'seq')  56.1 us
    psum x1, waiting for transfers between devices, body(): projected = lax.psum(partial_value, 'seq')  55.4 us
    psum x1, waiting for transfers between devices, body(): lax.psum(jnp.dot(mine_attended, thinker_out, preferred_element_type=jnp.f...  54.1 us
    psum x1, waiting for transfers between devices, body(): talker_in = lax.psum(pieces, 'seq')  51.4 us
    psum x1, blocking collectives, attend(): total, summed = lax.psum((total, summed), 'seq')  26.8 us
    dot_general x8, matrix products, attend(): jnp.einsum('bkgd,btkd->bkgt', query, key_four, preferred_element_type=jnp...  22.7 us
    dot_general x8, matrix products, attend(): jnp.einsum('bkgt,btkd->bkgd', weight_cached.astype(jnp.bfloat16), value_f...  16.5 us
  transfers between devices with their start and end apart: 5, of which 5 were waited for; matrix products, arithmetic and copies ran while one was open for 2% of the time, Pallas kernels for 0%

commit v1 on v0

v1 whole, which is shorter than its diff:
```python
import jax
import jax.numpy as jnp
from jax import lax
from jax.sharding import PartitionSpec as P

D = 3584
HQ = 28
HK = 4
HD = 128
TD = 896
AHQ = 12
AHK = 4
AHD = 128


EPSILON = 1e-06
THETA = 1000000.0
NEGATIVE = -1e30


def rotate(vectors, positions):
    width = vectors.shape[-1]
    half = width // 2
    freqs = jnp.exp(
        jnp.arange(half).astype(jnp.float32) * (-2.0 * jnp.log(jnp.float32(THETA)) / width)
    )
    angles = positions.astype(jnp.float32)[:, None] * freqs[None, :]
    cosine = jnp.cos(angles)[:, None, :]
    sine = jnp.sin(angles)[:, None, :]
    first = vectors[..., :half]
    second = vectors[..., half:]
    return jnp.concatenate(
        [first * cosine - second * sine, second * cosine + first * sine], axis=-1
    )


def attend(query, keys, values, new_keys, new_values, live, first):
    batch, steps, heads, group, width = query.shape
    count = keys.shape[1]
    scale = width ** (-0.5)
    key_four = keys.reshape(batch, count, heads, width)
    value_four = values.reshape(batch, count, heads, width)
    cached = (
        jnp.einsum("bskgd,btkd->bksgt", query, key_four, preferred_element_type=jnp.float32) * scale
    )
    fresh = (
        jnp.einsum("bskgd,bukd->bksgu", query, new_keys, preferred_element_type=jnp.float32) * scale
    )
    order = jnp.arange(steps)
    live_mask = live[:, None, None, None, :]
    fresh_mask = ((order[None, :] <= order[:, None]) & first)[None, None, :, None, :]
    cached = jnp.where(live_mask, cached, NEGATIVE)
    fresh = jnp.where(fresh_mask, fresh, NEGATIVE)
    peak = lax.pmax(jnp.maximum(cached.max(-1), fresh.max(-1)), "seq")
    weight_cached = jnp.where(live_mask, jnp.exp(cached - peak[..., None]), 0.0)
    weight_fresh = jnp.where(fresh_mask, jnp.exp(fresh - peak[..., None]), 0.0)
    total = weight_cached.sum(-1) + weight_fresh.sum(-1)
    summed = jnp.einsum(
        "bksgt,btkd->bksgd",
        weight_cached.astype(jnp.bfloat16),
        value_four,
        preferred_element_type=jnp.float32,
    ) + jnp.einsum(
        "bksgu,bukd->bksgd",
        weight_fresh.astype(jnp.bfloat16),
        new_values,
        preferred_element_type=jnp.float32,
    )
    total, summed = lax.psum((total, summed), "seq")
    out = (summed / total[..., None]).astype(jnp.bfloat16)
    return out.transpose(2, 0, 1, 3, 4).reshape(steps * batch, heads * group * width)


def body(
    thinker_input,
    thinker_gain,
    thinker_qkv,
    thinker_out,
    talker_proj,
    code_table,
    talker_gain,
    talker_qkv,
    talker_out,
    text_keys,
    text_values,
    audio_keys,
    audio_values,
    text_len,
    audio_len,
    text_pos,
    audio_pos,
    code_ids,
):
    steps, batch = thinker_input.shape[:2]
    rows = steps * batch
    index = lax.axis_index("seq")
    shards = lax.axis_size("seq")
    text_kv = HK * HD
    audio_q = AHQ * AHD
    audio_kv = AHK * AHD

    def live_of(cache, lengths):
        count = cache.shape[1]
        return (index * count + jnp.arange(count))[None, :] < lengths[:, None]

    def by_batch(heads):
        return heads.reshape((steps, batch) + heads.shape[1:]).swapaxes(0, 1)

    table_rows = code_table.shape[0]
    table_ids = index * table_rows + jnp.arange(table_rows)
    talker_cols = talker_out.shape[1] // shards
    out_slice = lax.dynamic_slice_in_dim(talker_out, index * talker_cols, talker_cols, 1)
    text_at = text_pos.T.reshape(rows)
    audio_at = audio_pos.T.reshape(rows)
    ids = code_ids.T.reshape(rows)

    inputs = thinker_input.reshape(rows, D).astype(jnp.float32)
    scaled = (inputs * thinker_gain).astype(jnp.bfloat16)
    n = thinker_qkv.shape[0]
    mine = lax.dynamic_slice_in_dim(scaled, index * n, n, 1)
    projected = lax.psum(jnp.dot(mine, thinker_qkv, preferred_element_type=jnp.float32), "seq")
    projected = projected * lax.rsqrt(jnp.sum(inputs * inputs, axis=-1) / D + EPSILON)[:, None]
    query = rotate(projected[:, :D].reshape(rows, HQ, HD), text_at).astype(jnp.bfloat16)
    key = rotate(projected[:, D : D + text_kv].reshape(rows, HK, HD), text_at).astype(jnp.bfloat16)
    value = projected[:, D + text_kv :].reshape(rows, HK, HD).astype(jnp.bfloat16)
    attended = attend(
        by_batch(query.reshape(rows, HK, HQ // HK, HD)),
        text_keys,
        text_values,
        by_batch(key),
        by_batch(value),
        live_of(text_keys, text_len),
        index == 0,
    )
    n = thinker_out.shape[0]
    mine = lax.dynamic_slice_in_dim(attended, index * n, n, 1)
    contribution = lax.psum(jnp.dot(mine, thinker_out, preferred_element_type=jnp.float32), "seq")
    hidden = (inputs + contribution).astype(jnp.bfloat16)
    picked = (ids[:, None] == table_ids[None, :]).astype(jnp.bfloat16)
    n = talker_proj.shape[0]
    mine = lax.dynamic_slice_in_dim(hidden, index * n, n, 1)
    talker_in = lax.psum(
        jnp.dot(mine, talker_proj, preferred_element_type=jnp.float32)
        + jnp.dot(picked, code_table, preferred_element_type=jnp.float32),
        "seq",
    )
    normed = (
        talker_in
        * lax.rsqrt(jnp.sum(talker_in * talker_in, axis=-1, keepdims=True) / TD + EPSILON)
        * talker_gain
    ).astype(jnp.bfloat16)
    spoken = jnp.dot(normed, talker_qkv, preferred_element_type=jnp.float32)
    query = rotate(spoken[:, :audio_q].reshape(rows, AHQ, AHD), audio_at).astype(jnp.bfloat16)
    key = rotate(
        spoken[:, audio_q : audio_q + audio_kv].reshape(rows, AHK, AHD), audio_at
    ).astype(jnp.bfloat16)
    value = spoken[:, audio_q + audio_kv :].reshape(rows, AHK, AHD).astype(jnp.bfloat16)
    heard = attend(
        by_batch(query.reshape(rows, AHK, AHQ // AHK, AHD)),
        audio_keys,
        audio_values,
        by_batch(key),
        by_batch(value),
        live_of(audio_keys, audio_len),
        index == 0,
    )
    residual = lax.dynamic_slice_in_dim(talker_in, index * talker_cols, talker_cols, 1)
    spoken_out = residual + jnp.dot(heard, out_slice, preferred_element_type=jnp.float32)
    return (
        hidden.reshape(steps, batch, D),
        spoken_out.astype(jnp.bfloat16).reshape(steps, batch, talker_cols),
    )


def solution(mesh):
    return jax.shard_map(
        body,
        mesh=mesh,
        in_specs=(
            P(None, "grp", None),
            P(),
            P("seq", None),
            P("seq", None),
            P("seq", None),
            P("seq", None),
            P(),
            P(),
            P(),
            P("grp", "seq", None),
            P("grp", "seq", None),
            P("grp", "seq", None),
            P("grp", "seq", None),
            P("grp"),
            P("grp"),
            P("grp", None),
            P("grp", None),
            P("grp", None),
        ),
        out_specs=(P(None, "grp", None), P(None, "grp", "seq")),
        check_vma=False,
    )
```

time: 539 us -> 398 us (0.74)
  matrix products: 106 us -> 28.7 us
  waiting for transfers between devices: 239 us -> 204 us
  other arithmetic: 51.8 us -> 19 us
  blocking collectives: 82.9 us -> 109 us
  local copies, waits for them, and re-layouts: 39.6 us -> 21.4 us
    dot_general x44 -> x11, matrix products: 86 us -> 20.7 us  [the longest x2 4.46 us: attend(): jnp.einsum('bksgt,btkd->bksgd', weight_cached.astype(jnp.bfloat16), value...]
    psum x2, waiting for transfers between devices: 78.6 us -> 49.8 us  [attend(): total, summed = lax.psum((total, summed), 'seq')]
    psum x1 -> x2, blocking collectives: 26.8 us -> 53.6 us  [attend(): total, summed = lax.psum((total, summed), 'seq')]
    scatter x14 -> x0, local copies, waits for them, and re-layouts: 14.5 us -> none  [the longest x4 4.92 us: body(): new_audio_values = new_audio_values.at[:, step].set(audio_value)]
    reshape x16 -> x8, local copies, waits for them, and re-layouts: 0.08 us -> 12.5 us  [the longest x2 4.42 us: attend(): key_four = keys.reshape(batch, count, heads, width)]
    concatenate x32 -> x8, local copies, waits for them, and re-layouts: 12 us -> 0.35 us  [rotate(): jnp.concatenate([first * cosine - second * sine, second * cosine + first...]
    reduce_sum x10 -> x4, other arithmetic: 14.3 us -> 4.78 us  [attend(): total = weight_cached.sum(-1) + weight_fresh.sum(-1)]
    convert_element_type x24 -> x5, local copies, waits for them, and re-layouts: 11.2 us -> 1.78 us  [the longest x1 0.63 us: body(): spoken[:, audio_q + audio_kv:].reshape(rows, AHK, AHD).astype(jnp.bfloat16)]
  transfers between devices with their start and end apart: 5 -> 5, of which waited for: 5 -> 5; matrix products, arithmetic and copies ran while one was open for 2% -> 4% of each run, Pallas kernels for 0% -> 0%
where the time goes in v1:
time: 398 us; the launch traced here: 397 us
  waiting for transfers between devices  204 us (51%)
  blocking collectives  109 us (27%)
  matrix products  28.7 us (7%)
  local copies, waits for them, and re-layouts  21.4 us (5%)
  other arithmetic  19 us (5%)
  between operations  14.3 us (4%)
    pmax x2, blocking collectives, attend(): peak = lax.pmax(jnp.maximum(cached.max(-1), fresh.max(-1)), 'seq')  55.5 us
    psum x1, waiting for transfers between devices, body(): lax.psum(jnp.dot(mine, thinker_out, preferred_element_type=jnp.float32),...  54.9 us
    psum x2, blocking collectives, attend(): total, summed = lax.psum((total, summed), 'seq')  53.6 us
    psum x1, waiting for transfers between devices, body(): lax.psum(jnp.dot(mine, thinker_qkv, preferred_element_type=jnp.float32),...  52.7 us
    psum x2, waiting for transfers between devices, attend(): total, summed = lax.psum((total, summed), 'seq')  49.8 us
    psum x1, waiting for transfers between devices, body(): lax.psum(jnp.dot(mine, talker_proj, preferred_element_type=jnp.float32) +...  46.7 us
  transfers between devices with their start and end apart: 5, of which 5 were waited for; matrix products, arithmetic and copies ran while one was open for 4% of the time, Pallas kernels for 0%

profile of v1, /device:TPU:0, one launch (start us, length us, event | category | flops | bytes accessed | tf_op | source)
XLA Modules:
  0.0 396.8 jit_solution(7313179571619321265)
XLA Ops:
  7.3 1.9 convert_bitcast_fusion
  9.9 3.9 fusion.45
  14.4 2.2 reshape.280
  16.6 2.2 reshape.282
  20.7 52.7 %all-reduce.6.cloned.1.call-done = f32[32,4608]{1,0:T(8,128)} async-done(((f32[32,4608]{1,0:T(8,128)}), f32[32,4608]{1,0:T(8,128)}) %all-reduce.6.cloned.1.call-update) | async-done | bytes 589840 | tf_op jit(solution)/shard_map/psum | solution.py:121
  77.5 1.9 reshape.279
  81.6 1.6 fusion.78
  83.1 2.1 fusion.79
  85.9 26.9 %pmax.14 = f32[8,4,4,7]{3,2,1,0:T(4,128)S(1)} all-reduce(f32[8,4,4,7]{3,2,1,0:T(4,128)} %max.10), channel_id=1, replica_groups=mesh['grp'=4,'seq'=8] {'seq'}, use_global_device_ids=true, to_apply=%region_4.5 | all-reduce | flops 896 | bytes 7168 | tf_op jit(solution)/shard_map/pmax | solution.py:54
  114.1 2.7 convolution_add_fusion
  119.6 27.2 %psum.51 = f32[8,4,4,7]{3,2,1,0:T(4,128)} all-reduce(f32[8,4,4,7]{3,2,1,0:T(4,128)S(1)} %add.108), channel_id=1, replica_groups=mesh['grp'=4,'seq'=8] {'seq'}, use_global_device_ids=true, to_apply=%region_8.9 | all-reduce | flops 896 | bytes 7168 | tf_op jit(solution)/shard_map/psum | solution.py:69
  146.8 24.5 %all-reduce.8.cloned.1.call-done = f32[8,4,4,7,128]{4,3,2,1,0:T(8,128)} async-done(((f32[8,4,4,7,128]{4,3,2,1,0:T(8,128)}), f32[8,4,4,7,128]{4,3,2,1,0:T(8,128)}) %all-reduce.8.cloned.1.call-update) | async-done | bytes 458768 | tf_op jit(solution)/shard_map/psum | solution.py:69
  174.5 54.9 %all-reduce.10.cloned.1.call-done = f32[32,3584]{1,0:T(8,128)} async-done(((f32[32,3584]{1,0:T(8,128)}), f32[32,3584]{1,0:T(8,128)}) %all-reduce.10.cloned.1.call-update) | async-done | bytes 458768 | tf_op jit(solution)/shard_map/psum | solution.py:137
  232.5 2.6 convolution_add_fusion.2
  235.2 2.2 reshape.286
  237.4 2.2 reshape.288
  239.6 46.7 %all-reduce.12.cloned.1.call-done = f32[32,896]{1,0:T(8,128)} async-done(((f32[32,896]{1,0:T(8,128)}), f32[32,896]{1,0:T(8,128)}) %all-reduce.12.cloned.1.call-update) | async-done | bytes 114704 | tf_op jit(solution)/shard_map/psum | solution.py:142
  287.3 3.3 fusion.38
  297.7 2.8 fusion.80
  300.5 28.6 %pmax.15 = f32[8,4,4,3]{2,3,1,0:T(4,128)S(1)} all-reduce(f32[8,4,4,3]{2,3,1,0:T(4,128)S(1)} %max.11), channel_id=1, replica_groups=mesh['grp'=4,'seq'=8] {'seq'}, use_global_device_ids=true, to_apply=%region_14.15 | all-reduce | flops 384 | bytes 3072 | tf_op jit(solution)/shard_map/pmax | solution.py:54
  331.4 1.8 fusion.5
  335.4 26.4 %psum.55 = f32[8,4,4,3]{2,3,1,0:T(4,128)S(1)} all-reduce(f32[8,4,4,3]{2,3,1,0:T(4,128)S(1)} %add.119), channel_id=1, replica_groups=mesh['grp'=4,'seq'=8] {'seq'}, use_global_device_ids=true, to_apply=%region_18.19 | all-reduce | flops 384 | bytes 3072 | tf_op jit(solution)/shard_map/psum | solution.py:69
  361.8 25.3 %all-reduce.14.cloned.1.call-done = f32[8,4,4,3,128]{4,2,3,1,0:T(4,128)} async-done(((f32[8,4,4,3,128]{4,2,3,1,0:T(4,128)}), f32[8,4,4,3,128]{4,2,3,1,0:T(4,128)}) %all-reduce.14.cloned.1.call-update) | async-done | bytes 196624 | tf_op jit(solution)/shard_map/psum | solution.py:69
  388.2 2.1 fusion.4
  (117 shorter events, 34.1 us)
Async XLA Ops:
  7.2 165.6 %copy-start = (bf16[448,3584]{1,0:T(8,128)(2,1)S(1)}, bf16[448,3584]{1,0:T(8,128)(2,1)}, u32[]{:S(2)}) copy-start(bf16[448,3584]{1,0:T(8,128)(2,1)} %param.21) | copy-start | bytes 9633796
  7.2 6.8 %copy-start.2 = (bf16[4,8,3584]{2,1,0:T(8,128)(2,1)S(1)}, bf16[4,8,3584]{2,1,0:T(8,128)(2,1)}, u32[]{:S(2)}) copy-start(bf16[4,8,3584]{2,1,0:T(8,128)(2,1)} %param.18) | copy-start | bytes 688132
  7.2 6.9 %copy-start.15 = (s32[8,4]{0,1:T(4,128)S(1)}, s32[8,4]{0,1:T(4,128)}, u32[]{:S(2)}) copy-start(s32[8,4]{0,1:T(4,128)} %param.33) | copy-start | bytes 388
  7.2 7.0 %copy-start.16 = (s32[8,4]{0,1:T(4,128)S(1)}, s32[8,4]{0,1:T(4,128)}, u32[]{:S(2)}) copy-start(s32[8,4]{0,1:T(4,128)} %param.34) | copy-start | bytes 388
  7.2 66.2 %all-reduce.6.cloned.1.call-start = ((), (), s32[]{:S(2)}) async-start(), calls=%async_computation | async-start | bytes 1179648 | tf_op jit(solution)/shard_map/psum | solution.py:121
  13.8 4.9 %copy-start.17 = (s32[8]{0:T(128)S(1)}, s32[8]{0:T(128)}, u32[]{:S(2)}) copy-start(s32[8]{0:T(128)} %param.32) | copy-start | bytes 100
  13.8 4.9 %copy-start.18 = (s32[8]{0:T(128)S(1)}, s32[8]{0:T(128)}, u32[]{:S(2)}) copy-start(s32[8]{0:T(128)} %param.31) | copy-start | bytes 100
  13.9 157.5 %all-reduce.8.cloned.1.call-start = ((), (), s32[]{:S(2)}) async-start(), calls=%async_computation.1 | async-start | bytes 1048576 | tf_op jit(solution)/shard_map/psum | solution.py:69
  79.4 2.1 copy-start.1
  79.4 2.1 copy-start.7
  79.4 3.7 copy-start.9
  85.2 31.6 %copy-start.10 = (pred[4,4]{1,0:T(4,128)(4,1)S(1)}, pred[4,4]{1,0:T(4,128)(4,1)}, u32[]{:S(2)}) copy-start(pred[4,4]{1,0:T(4,128)(4,1)} %fusion.65) | copy-start | bytes 52
  85.2 32.9 %copy-start.8 = (pred[8,128]{1,0:T(8,128)(4,1)S(1)}, pred[8,128]{1,0:T(8,128)(4,1)}, u32[]{:S(2)}) copy-start(pred[8,128]{1,0:T(8,128)(4,1)} %get-tuple-element.23) | copy-start | bytes 3076
  116.8 112.5 %all-reduce.10.cloned.1.call-start = ((), (), s32[]{:S(2)}) async-start(), calls=%async_computation.2 | async-start | bytes 917504 | tf_op jit(solution)/shard_map/psum | solution.py:137
  118.1 56.3 %copy-start.14 = (s32[8,4]{0,1:T(4,128)S(1)}, s32[8,4]{0,1:T(4,128)}, u32[]{:S(2)}) copy-start(s32[8,4]{0,1:T(4,128)} %param.35) | copy-start | bytes 388
  174.3 111.9 %all-reduce.12.cloned.1.call-start = ((), (), s32[]{:S(2)}) async-start(), calls=%async_computation.3 | async-start | bytes 229376 | tf_op jit(solution)/shard_map/psum | solution.py:142
  230.4 0.7 copy-start.3
  232.5 54.8 %copy-start.12 = (f32[896]{0:T(1024)S(1)}, f32[896]{0:T(1024)}, u32[]{:S(2)}) copy-start(f32[896]{0:T(1024)} %param.24) | copy-start | bytes 10756
  235.2 151.9 %all-reduce.14.cloned.1.call-start = ((), (), s32[]{:S(2)}) async-start(), calls=%async_computation.4 | async-start | bytes 393216 | tf_op jit(solution)/shard_map/psum | solution.py:69
  293.9 1.0 copy-start.5
  294.7 34.5 %copy-start.11 = (pred[4,4]{1,0:T(4,128)(4,1)S(1)}, pred[4,4]{1,0:T(4,128)(4,1)}, u32[]{:S(2)}) copy-start(pred[4,4]{1,0:T(4,128)(4,1)} %fusion.65) | copy-start | bytes 52
  294.7 36.6 %copy-start.13 = (pred[8,128]{1,0:T(8,128)(4,1)S(1)}, pred[8,128]{1,0:T(8,128)(4,1)}, u32[]{:S(2)}) copy-start(pred[8,128]{1,0:T(8,128)(4,1)} %get-tuple-element.22) | copy-start | bytes 3076
  294.7 38.4 %copy-start.4 = (bf16[4,8,4,128]{3,1,2,0:T(8,128)(2,1)S(1)}, bf16[4,8,4,128]{3,1,2,0:T(8,128)(2,1)}, u32[]{:S(2)}) copy-start(bf16[4,8,4,128]{3,1,2,0:T(8,128)(2,1)} %fusion.48) | copy-start | bytes 98308
  294.9 0.6 copy-start.6
Sparse Core Ops, SparseCore 0:
  14.0 59.3 all-reduce.5
  116.9 54.3 all-reduce.7
  174.4 54.8 all-reduce.9
  235.3 50.9 all-reduce.11
  334.2 52.8 all-reduce.13

commit v2 on v1

--- a/solution.py
+++ b/solution.py
@@ -1,6 +1,10 @@
+import functools
+
 import jax
 import jax.numpy as jnp
 from jax import lax
+from jax.experimental import pallas as pl
+from jax.experimental.pallas import tpu as pltpu
 from jax.sharding import PartitionSpec as P
 
 D = 3584
@@ -34,7 +38,128 @@
     )
 
 
-def attend(query, keys, values, new_keys, new_values, live, first):
+LANES = 128
+
+
+def greet(n, me):
+    barrier = pltpu.get_barrier_semaphore()
+    for off in range(1, n):
+        pl.semaphore_signal(
+            barrier,
+            inc=1,
+            device_id={"seq": lax.rem(me + off, n)},
+            device_id_type=pl.DeviceIdType.MESH,
+        )
+    return barrier
+
+
+def remote(n, me, off, src, dst, send_sem, recv_sem):
+    return pltpu.make_async_remote_copy(
+        src_ref=src,
+        dst_ref=dst,
+        send_sem=send_sem.at[off - 1],
+        recv_sem=recv_sem.at[off - 1],
+        device_id={"seq": lax.rem(me + off, n)},
+        device_id_type=pl.DeviceIdType.MESH,
+    )
+
+
+def sum_kernel(n, per, x_ref, o_ref, sent, landed, whole, send_one, recv_one, send_two, recv_two):
+    me = lax.axis_index("seq")
+    barrier = greet(n, me)
+    blocks = x_ref.shape[1] // LANES
+    for j in range(blocks):
+        sent[j] = x_ref[:, j * LANES : (j + 1) * LANES].astype(sent.dtype)
+    for j in range(blocks, n * per):
+        sent[j] = jnp.zeros(sent.shape[1:], sent.dtype)
+    pl.semaphore_wait(barrier, n - 1)
+    out = []
+    for off in range(1, n):
+        part = pl.ds(lax.rem(me + off, n) * per, per)
+        out.append(remote(n, me, off, sent.at[part], landed.at[off - 1], send_one, recv_one))
+        out[-1].start()
+    mine = pl.ds(me * per, per)
+    total = sent[mine].astype(jnp.float32)
+    for off in range(1, n):
+        out[off - 1].wait_recv()
+        total = total + landed[off - 1].astype(jnp.float32)
+    whole[mine] = total.astype(whole.dtype)
+    back = []
+    for off in range(1, n):
+        back.append(remote(n, me, off, whole.at[mine], whole.at[mine], send_two, recv_two))
+        back[-1].start()
+    for copy in out:
+        copy.wait_send()
+    for copy in back:
+        copy.wait_recv()
+    for j in range(blocks):
+        o_ref[:, j * LANES : (j + 1) * LANES] = whole[j].astype(o_ref.dtype)
+    for copy in back:
+        copy.wait_send()
+
+
+def sum_over(x, n, ident):
+    rows, columns = x.shape
+    per = -(-(columns // LANES) // n)
+    vmem = pl.BlockSpec(memory_space=pltpu.VMEM)
+    dma = pltpu.SemaphoreType.DMA((n - 1,))
+    return pl.pallas_call(
+        functools.partial(sum_kernel, n, per),
+        out_shape=jax.ShapeDtypeStruct(x.shape, jnp.float32),
+        in_specs=[vmem],
+        out_specs=vmem,
+        scratch_shapes=[
+            pltpu.VMEM((n * per, rows, LANES), jnp.bfloat16),
+            pltpu.VMEM((n - 1, per, rows, LANES), jnp.bfloat16),
+            pltpu.VMEM((n * per, rows, LANES), jnp.bfloat16),
+            dma,
+            dma,
+            dma,
+            dma,
+        ],
+        compiler_params=pltpu.CompilerParams(
+            collective_id=ident, has_side_effects=True, vmem_limit_bytes=16 * 2**20
+        ),
+    )(x)
+
+
+def peak_kernel(n, x_ref, o_ref, landed, send_sem, recv_sem):
+    me = lax.axis_index("seq")
+    barrier = greet(n, me)
+    pl.semaphore_wait(barrier, n - 1)
+    out = []
+    for off in range(1, n):
+        out.append(remote(n, me, off, x_ref, landed.at[off - 1], send_sem, recv_sem))
+        out[-1].start()
+    top = x_ref[...]
+    for off in range(1, n):
+        out[off - 1].wait_recv()
+        top = jnp.maximum(top, landed[off - 1])
+    o_ref[...] = top
+    for copy in out:
+        copy.wait_send()
+
+
+def peak_over(x, n, ident):
+    tile = 8 * LANES
+    padded = -(-x.size // tile) * tile
+    flat = jnp.pad(x.reshape(-1), (0, padded - x.size)).reshape(-1, LANES)
+    vmem = pl.BlockSpec(memory_space=pltpu.VMEM)
+    dma = pltpu.SemaphoreType.DMA((n - 1,))
+    top = pl.pallas_call(
+        functools.partial(peak_kernel, n),
+        out_shape=jax.ShapeDtypeStruct(flat.shape, jnp.float32),
+        in_specs=[vmem],
+        out_specs=vmem,
+        scratch_shapes=[pltpu.VMEM((n - 1,) + flat.shape, jnp.float32), dma, dma],
+        compiler_params=pltpu.CompilerParams(
+            collective_id=ident, has_side_effects=True, vmem_limit_bytes=16 * 2**20
+        ),
+    )(flat)
+    return top.reshape(-1)[: x.size].reshape(x.shape)
+
+
+def attend(query, keys, values, new_keys, new_values, live, first, shards, ident):
     batch, steps, heads, group, width = query.shape
     count = keys.shape[1]
     scale = width ** (-0.5)
@@ -51,7 +176,7 @@
     fresh_mask = ((order[None, :] <= order[:, None]) & first)[None, None, :, None, :]
     cached = jnp.where(live_mask, cached, NEGATIVE)
     fresh = jnp.where(fresh_mask, fresh, NEGATIVE)
-    peak = lax.pmax(jnp.maximum(cached.max(-1), fresh.max(-1)), "seq")
+    peak = peak_over(jnp.maximum(cached.max(-1), fresh.max(-1)), shards, ident)
     weight_cached = jnp.where(live_mask, jnp.exp(cached - peak[..., None]), 0.0)
     weight_fresh = jnp.where(fresh_mask, jnp.exp(fresh - peak[..., None]), 0.0)
     total = weight_cached.sum(-1) + weight_fresh.sum(-1)
@@ -66,9 +191,14 @@
         new_values,
         preferred_element_type=jnp.float32,
     )
-    total, summed = lax.psum((total, summed), "seq")
-    out = (summed / total[..., None]).astype(jnp.bfloat16)
-    return out.transpose(2, 0, 1, 3, 4).reshape(steps * batch, heads * group * width)
+    rows, count = steps * batch, heads * group
+    totals = total.transpose(2, 0, 1, 3).reshape(rows, count)
+    totals = jnp.pad(totals, ((0, 0), (0, -count % LANES)))
+    values = summed.transpose(2, 0, 1, 3, 4).reshape(rows, count * width)
+    both = sum_over(jnp.concatenate([values, totals], axis=1), shards, ident + 1)
+    out = both[:, : count * width].reshape(rows, count, width)
+    total = both[:, count * width : count * width + count]
+    return (out / total[:, :, None]).astype(jnp.bfloat16).reshape(rows, count * width)
 
 
 def body(
@@ -118,7 +248,9 @@
     scaled = (inputs * thinker_gain).astype(jnp.bfloat16)
     n = thinker_qkv.shape[0]
     mine = lax.dynamic_slice_in_dim(scaled, index * n, n, 1)
-    projected = lax.psum(jnp.dot(mine, thinker_qkv, preferred_element_type=jnp.float32), "seq")
+    projected = sum_over(
+        jnp.dot(mine, thinker_qkv, preferred_element_type=jnp.float32), shards, 0
+    )
     projected = projected * lax.rsqrt(jnp.sum(inputs * inputs, axis=-1) / D + EPSILON)[:, None]
     query = rotate(projected[:, :D].reshape(rows, HQ, HD), text_at).astype(jnp.bfloat16)
     key = rotate(projected[:, D : D + text_kv].reshape(rows, HK, HD), text_at).astype(jnp.bfloat16)
@@ -131,18 +263,23 @@
         by_batch(value),
         live_of(text_keys, text_len),
         index == 0,
+        shards,
+        1,
     )
     n = thinker_out.shape[0]
     mine = lax.dynamic_slice_in_dim(attended, index * n, n, 1)
-    contribution = lax.psum(jnp.dot(mine, thinker_out, preferred_element_type=jnp.float32), "seq")
+    contribution = sum_over(
+        jnp.dot(mine, thinker_out, preferred_element_type=jnp.float32), shards, 3
+    )
     hidden = (inputs + contribution).astype(jnp.bfloat16)
     picked = (ids[:, None] == table_ids[None, :]).astype(jnp.bfloat16)
     n = talker_proj.shape[0]
     mine = lax.dynamic_slice_in_dim(hidden, index * n, n, 1)
-    talker_in = lax.psum(
+    talker_in = sum_over(
         jnp.dot(mine, talker_proj, preferred_element_type=jnp.float32)
         + jnp.dot(picked, code_table, preferred_element_type=jnp.float32),
-        "seq",
+        shards,
+        4,
     )
     normed = (
         talker_in
@@ -163,6 +300,8 @@
         by_batch(value),
         live_of(audio_keys, audio_len),
         index == 0,
+        shards,
+        5,
     )
     residual = lax.dynamic_slice_in_dim(talker_in, index * talker_cols, talker_cols, 1)
     spoken_out = residual + jnp.dot(heard, out_slice, preferred_element_type=jnp.float32)

time: 398 us -> 159 us (0.40)
  waiting for transfers between devices: 204 us -> 0 us
  blocking collectives: 109 us -> 0 us
  Pallas kernels: 0 us -> 85.9 us
  between operations: 14.3 us -> 1.28 us
  local copies, waits for them, and re-layouts: 21.4 us -> 30.4 us
  matrix products: 28.7 us -> 23.2 us
    psum x5 -> x0, waiting for transfers between devices: 204 us -> none  [the longest x1 54.9 us: body(): lax.psum(jnp.dot(mine, thinker_out, preferred_element_type=jnp.float32),...]
    pallas_call x0 -> x7, Pallas kernels: none -> 85.9 us  [the longest x5 72.4 us: sum_over(): pl.pallas_call(functools.partial(sum_kernel, n, per), out_shape=jax.Shape...]
    pmax x2 -> x0, blocking collectives: 55.5 us -> none  [attend(): peak = lax.pmax(jnp.maximum(cached.max(-1), fresh.max(-1)), 'seq')]
    psum x2 -> x0, blocking collectives: 53.6 us -> none  [attend(): total, summed = lax.psum((total, summed), 'seq')]
  transfers between devices with their start and end apart: 5 -> 0, of which waited for: 5 -> 0; matrix products, arithmetic and copies ran while one was open for 4% -> 0% of each run, Pallas kernels for 0% -> 0%
where the time goes in v2:
time: 159 us; the launch traced here: 158 us
  Pallas kernels  85.9 us (54%)
  local copies, waits for them, and re-layouts  30.4 us (19%)
  matrix products  23.2 us (15%)
  other arithmetic  17.1 us (11%)
    pallas_call x5, Pallas kernels, sum_over(): pl.pallas_call(functools.partial(sum_kernel, n, per), out_shape=jax.Shape...  72.4 us
    pallas_call x2, Pallas kernels, peak_over(): pl.pallas_call(functools.partial(peak_kernel, n), out_shape=jax.ShapeDtyp...  13.5 us
    dot_general x2, matrix products, attend(): jnp.einsum('bskgd,btkd->bksgt', query, key_four, preferred_element_type=j...  5.67 us
    reshape x2, local copies, waits for them, and re-layouts, attend(): value_four = values.reshape(batch, count, heads, width)  4.29 us
    reshape x2, local copies, waits for them, and re-layouts, attend(): key_four = keys.reshape(batch, count, heads, width)  4.28 us
    dot_general x2, matrix products, attend(): jnp.einsum('bskgd,bukd->bksgu', query, new_keys, preferred_element_type=j...  4.12 us
    dot_general x2, matrix products, attend(): jnp.einsum('bksgt,btkd->bksgd', weight_cached.astype(jnp.bfloat16), value...  3.78 us
    reduce_sum x3, other arithmetic, attend(): total = weight_cached.sum(-1) + weight_fresh.sum(-1)  3.69 us

profile of v2, /device:TPU:0, one launch (start us, length us, event | category | flops | bytes accessed | tf_op | source)
XLA Modules:
  0.0 157.9 jit_solution(17844005791161744204)
XLA Ops:
  1.2 1.6 %eq.20 = s32[32]{0:T(128)} reshape(s32[4,8]{1,0:T(4,128)} %bitcast.126) | data formatting | bytes 256 | tf_op jit(solution)/shard_map/eq | solution.py:275
  9.5 3.1 %fusion.48.x_ref = f32[32,4608]{1,0:T(8,128)S(1)} fusion(bf16[448,4608]{1,0:T(8,128)(2,1)} %param.20, f32[32,3584]{1,0:T(8,128)S(1)} %convert_bitcast_fusion, s32[]{:T(128)S(6)} %select_n.37, f32[448]{0:T(512)S(1)} %dynamic-slice), kind=kOutput, calls=%fused_computation.84 | convolution fusion | flops 132149248 | bytes 4786180 | tf_op jit(solution)/shard_map/dot_general | solution.py:252
  12.5 18.4 %shard_map.185 = f32[32,4608]{1,0:T(8,128)S(1)} custom-call(f32[32,4608]{1,0:T(8,128)S(1)} %fusion.48.x_ref), custom_call_target="tpu_custom_call" | custom-call | tf_op jit(solution)/shard_map/pallas_call | solution.py:106
  32.5 1.9 %reshape.311 = f32[32,28,128]{2,1,0:T(8,128)} reshape(f32[32,3584]{1,0:T(8,128)} %slice.84) | data formatting | bytes 917504 | tf_op jit(solution)/shard_map/reshape | solution.py:255
  36.7 2.7 %fusion.82 = (f32[8,4,4,7]{3,2,1,0:T(4,128)}, f32[8,4,4,7,4]{3,4,2,1,0:T(4,128)S(1)}) fusion(bf16[4,8,4,64]{3,0,2,1:T(4,128)(2,1)S(1)} %copy.103, bf16[4,8,4,64]{3,0,2,1:T(4,128)(2,1)S(1)} %copy.102, bf16[4,8,4,7,64]{4,3,0,2,1:T(8,128)(2,1)S(1)} %copy.98, bf16[4,8,4,7,64]{4,3,0,2,1:T(8,128)(2,1)S(1)} %copy.97, pred[4,4]{1,0:T(4,128)(4,1)} %fusion.68), kind=kOutput, calls=%fused_computation.134 | convolution fusion | flops 1451648 | bytes 280080 | tf_op jit(solution)/shard_map/bskgd,bukd->bksgu/dot_general | solution.py:172
  39.4 2.1 %reshape.312 = bf16[8,128,4,128]{3,2,1,0:T(4,128)(2,1)} reshape(bf16[8,128,512]{2,1,0:T(8,128)(2,1)} %param.27) | data formatting | bytes 2097152 | tf_op jit(solution)/shard_map/reshape | solution.py:166
  41.6 2.9 %fusion.81 = (f32[8,4,4,7]{3,2,1,0:T(4,128)S(1)}, f32[8,4,4,7,128]{4,3,2,1,0:T(8,128)}) fusion(bf16[8,128,4,128,1]{3,2,1,0,4:T(4,128)(2,1)} %bitcast.113, bf16[4,8,4,7,64]{4,3,0,2,1:T(8,128)(2,1)} %copy-done.4, bf16[4,8,4,7,64]{4,3,0,2,1:T(8,128)(2,1)} %copy-done.3, pred[8,128]{1,0:T(8,128)(4,1)S(1)} %get-tuple-element.23), kind=kOutput, calls=%fused_computation.133 | convolution fusion | flops 30162048 | bytes 1741312 | tf_op jit(solution)/shard_map/bskgd,btkd->bksgt/dot_general | solution.py:169
  45.6 7.9 %shard_map.186 = f32[8,128]{1,0:T(8,128)S(1)} custom-call(f32[8,128]{1,0:T(8,128)S(1)} %pad_bitcast_fusion.1.x_ref), custom_call_target="tpu_custom_call" | custom-call | tf_op jit(solution)/shard_map/pallas_call | solution.py:149
  56.8 1.5 reshape.336
  58.3 1.9 %fusion.24 = f32[8,4,4,7,128]{4,3,2,1,0:T(8,128)} fusion(f32[8,4,4,7,4]{3,4,2,1,0:T(4,128)S(1)} %get-tuple-element.27, f32[8,4,4,7]{3,2,1,0:T(4,128)S(1)} %sub.50, pred[4,4]{1,0:T(4,128)(4,1)} %fusion.68, bf16[4,8,4,128]{3,1,2,0:T(8,128)(2,1)} %fusion.50), kind=kOutput, calls=%fused_computation.48 | convolution fusion | flops 928256 | bytes 509456 | tf_op jit(solution)/shard_map/bksgu,bukd->bksgd/dot_general | solution.py:188
  60.2 2.2 %reshape.315 = bf16[8,128,4,128]{3,2,1,0:T(4,128)(2,1)} reshape(bf16[8,128,512]{2,1,0:T(8,128)(2,1)} %param.28) | data formatting | bytes 2097152 | tf_op jit(solution)/shard_map/reshape | solution.py:167
  62.4 2.0 %fusion = f32[4,8,4,7,128]{4,3,0,2,1:T(8,128)S(1)} fusion(f32[8,4,4,7,128]{4,3,2,1,0:T(8,128)} %fusion.24, bf16[8,128,4,128,1]{3,2,1,0,4:T(4,128)(2,1)} %bitcast.112, f32[8,4,4,7,128]{4,3,2,1,0:T(8,128)} %get-tuple-element.25, f32[8,4,4,7]{3,2,1,0:T(4,128)S(1)} %sub.50, pred[8,128]{1,0:T(8,128)(4,1)S(1)} %get-tuple-element.23), kind=kOutput, calls=%fused_computation.1 | convolution fusion | flops 29818880 | bytes 2429440 | tf_op jit(solution)/shard_map/bksgt,btkd->bksgd/dot_general | solution.py:183
  64.7 15.2 %shard_map.187 = f32[32,3712]{1,0:T(8,128)S(1)} custom-call(f32[32,3712]{1,0:T(8,128)S(1)} %select_maximum_fusion.x_ref), custom_call_target="tpu_custom_call" | custom-call | tf_op jit(solution)/shard_map/pallas_call | solution.py:106
  81.2 16.2 %shard_map.188 = f32[32,3584]{1,0:T(8,128)S(1)} custom-call(f32[32,3584]{1,0:T(8,128)S(1)} %fusion.51.x_ref), custom_call_target="tpu_custom_call" | custom-call | tf_op jit(solution)/shard_map/pallas_call | solution.py:106
  98.3 11.9 %shard_map.189 = f32[32,896]{1,0:T(8,128)S(1)} custom-call(f32[32,896]{1,0:T(8,128)S(1)} %convolution_add_fusion.2.x_ref), custom_call_target="tpu_custom_call" | custom-call | tf_op jit(solution)/shard_map/pallas_call | solution.py:106
  112.6 1.5 reshape.321
  121.7 2.1 %reshape.320 = bf16[8,128,4,128]{3,2,1,0:T(4,128)(2,1)} reshape(bf16[8,128,512]{2,1,0:T(8,128)(2,1)} %param.29) | data formatting | bytes 2097152 | tf_op jit(solution)/shard_map/reshape | solution.py:166
  123.8 2.7 %fusion.83 = (f32[8,4,4,3]{2,3,1,0:T(4,128)S(1)}, f32[8,4,4,3,128]{4,2,3,1,0:T(4,128)}) fusion(bf16[8,128,4,128,1]{3,2,1,0,4:T(4,128)(2,1)} %bitcast.116, bf16[4,8,4,3,64]{4,0,3,2,1:T(4,128)(2,1)} %copy-done.11, bf16[4,8,4,3,64]{4,0,3,2,1:T(4,128)(2,1)} %copy-done.10, pred[8,128]{1,0:T(8,128)(4,1)S(1)} %copy-done.14), kind=kOutput, calls=%fused_computation.135 | convolution fusion | flops 12926592 | bytes 1346048 | tf_op jit(solution)/shard_map/bskgd,btkd->bksgt/dot_general | solution.py:169
  127.2 5.6 %shard_map.190 = f32[8,128]{1,0:T(8,128)S(1)} custom-call(f32[8,128]{1,0:T(8,128)S(1)} %pad_bitcast_fusion.x_ref), custom_call_target="tpu_custom_call" | custom-call | tf_op jit(solution)/shard_map/pallas_call | solution.py:149
  133.2 2.0 %fusion.67 = (bf16[8,4,4,3,4]{0,4,3,2,1:T(4,128)(2,1)}, f32[8,4,4,3]{0,3,2,1:T(4,128)}) fusion(f32[8,4,4,3]{0,3,2,1:T(4,128)S(1)} %copy.123, f32[8,4,4,3,4]{0,4,3,2,1:T(4,128)S(1)} %copy.118, pred[4,4]{1,0:T(4,128)(4,1)} %fusion.68), kind=kLoop, calls=%fused_computation.107 | loop fusion | flops 8832 | bytes 12304 | tf_op jit(solution)/shard_map/convert_element_type | solution.py:190
  140.8 2.1 %reshape.323 = bf16[8,128,4,128]{3,2,1,0:T(4,128)(2,1)} reshape(bf16[8,128,512]{2,1,0:T(8,128)(2,1)} %param.30) | data formatting | bytes 2097152 | tf_op jit(solution)/shard_map/reshape | solution.py:167
  142.9 1.8 %fusion.7 = f32[8,4,4,3,128]{4,2,3,1,0:T(4,128)S(1)} fusion(bf16[8,128,4,128,1]{3,2,1,0,4:T(4,128)(2,1)} %bitcast.117, f32[8,4,4,3,128]{4,2,3,1,0:T(4,128)} %get-tuple-element.29, f32[8,4,4,3]{2,3,1,0:T(4,128)S(1)} %copy.121, pred[8,128]{1,0:T(8,128)(4,1)} %get-tuple-element.22), kind=kOutput, calls=%fused_computation.14 | convolution fusion | flops 12730368 | bytes 1444352 | tf_op jit(solution)/shard_map/bksgt,btkd->bksgd/dot_general | solution.py:183
  145.0 10.7 %shard_map.191 = f32[32,1664]{1,0:T(8,128)S(1)} custom-call(f32[32,1664]{1,0:T(8,128)S(1)} %select_maximum_fusion.1.x_ref), custom_call_target="tpu_custom_call" | custom-call | tf_op jit(solution)/shard_map/pallas_call | solution.py:106
  155.8 2.1 %fusion.6 = bf16[4,8,112]{2,1,0:T(8,128)(2,1)} fusion(bf16[1536,896]{1,0:T(8,128)(2,1)} %param.26, s32[]{:T(128)S(6)} %select_n.42, f32[4,8,12,128]{3,2,1,0:T(8,128)S(1)} %bitcast.125, f32[32,1664]{1,0:T(8,128)S(1)} %shard_map.191, f32[32,896]{1,0:T(8,128)S(1)} %shard_map.189), kind=kOutput, calls=%fused_computation.13 | convolution fusion | flops 11115520 | bytes 876544 | tf_op jit(solution)/shard_map/dot_general | solution.py:307
  (124 shorter events, 34.4 us)
Async XLA Ops:
  0.6 79.8 %copy-start = (bf16[448,3584]{1,0:T(8,128)(2,1)S(1)}, bf16[448,3584]{1,0:T(8,128)(2,1)}, u32[]{:S(2)}) copy-start(bf16[448,3584]{1,0:T(8,128)(2,1)} %param.21) | copy-start | bytes 9633796
  36.1 0.7 copy-start.3
  36.7 2.7 %copy-start.4 = (bf16[4,8,4,7,64]{4,3,0,2,1:T(8,128)(2,1)}, bf16[4,8,4,7,64]{4,3,0,2,1:T(8,128)(2,1)S(1)}, u32[]{:S(2)}) copy-start(bf16[4,8,4,7,64]{4,3,0,2,1:T(8,128)(2,1)S(1)} %copy.98) | copy-start | bytes 344068
  60.2 4.4 %copy-start.12 = (f32[32,28]{1,0:T(8,128)S(1)}, f32[32,28]{1,0:T(8,128)}, u32[]{:S(2)}) copy-start(f32[32,28]{1,0:T(8,128)} %reshape.336) | copy-start | bytes 10756
  79.9 17.5 %copy-start.1 = (bf16[4,8,3584]{2,1,0:T(8,128)(2,1)S(1)}, bf16[4,8,3584]{2,1,0:T(8,128)(2,1)}, u32[]{:S(2)}) copy-start(bf16[4,8,3584]{2,1,0:T(8,128)(2,1)} %param.18) | copy-start | bytes 688132
  80.0 30.4 %slice-start = ((s8[4587520]{0:T(1024)(128)(4,1)}), s8[4194304]{0:T(1024)(128)(4,1)S(1)}, s32[]{:S(2)}) async-start(s8[4587520]{0:T(1024)(128)(4,1)} %bitcast.110), calls=%async_computation | async-start | bytes 8388608
  80.2 17.3 %copy-start.5 = (bf16[448,896]{1,0:T(8,128)(2,1)S(1)}, bf16[448,896]{1,0:T(8,128)(2,1)}, u32[]{:S(2)}) copy-start(bf16[448,896]{1,0:T(8,128)(2,1)} %param.22) | copy-start | bytes 2408452
  80.5 17.3 %copy-start.2 = (bf16[1056,896]{1,0:T(8,128)(2,1)S(1)}, bf16[1056,896]{1,0:T(8,128)(2,1)}, u32[]{:S(2)}) copy-start(bf16[1056,896]{1,0:T(8,128)(2,1)} %param.23) | copy-start | bytes 5677060
  80.5 17.3 %copy-start.15 = (s32[32]{0:T(128)S(1)}, s32[32]{0:T(128)}, u32[]{:S(2)}) copy-start(s32[32]{0:T(128)} %eq.20) | copy-start | bytes 388
  80.5 29.9 %slice-start.1 = ((s8[4587520]{0:T(1024)(128)(4,1)}), s8[393216]{0:T(1024)(128)(4,1)S(1)}, s32[]{:S(2)}) async-start(s8[4587520]{0:T(1024)(128)(4,1)} %bitcast.110), calls=%async_computation.1 | async-start | bytes 786432
  81.2 29.2 %copy-start.13 = (f32[896]{0:T(1024)S(1)}, f32[896]{0:T(1024)}, u32[]{:S(2)}) copy-start(f32[896]{0:T(1024)} %param.24) | copy-start | bytes 10756
  97.5 13.9 %copy-start.6 = (bf16[32,3584]{1,0:T(8,128)(2,1)}, bf16[32,3584]{1,0:T(8,128)(2,1)S(1)}, u32[]{:S(2)}) copy-start(bf16[32,3584]{1,0:T(8,128)(2,1)S(1)} %add_convert_fusion.1) | copy-start | bytes 688132
  110.2 4.6 %copy-start.7 = (f32[32,64]{1,0:T(8,128)S(1)}, f32[32,64]{1,0:T(8,128)}, u32[]{:S(2)}) copy-start(f32[32,64]{1,0:T(8,128)} %get-tuple-element.16) | copy-start | bytes 24580
  110.2 4.6 %copy-start.8 = (f32[32,64]{1,0:T(8,128)S(1)}, f32[32,64]{1,0:T(8,128)}, u32[]{:S(2)}) copy-start(f32[32,64]{1,0:T(8,128)} %get-tuple-element.17) | copy-start | bytes 24580
  116.1 1.2 copy-start.10
  117.1 6.7 %copy-start.14 = (pred[8,128]{1,0:T(8,128)(4,1)S(1)}, pred[8,128]{1,0:T(8,128)(4,1)}, u32[]{:S(2)}) copy-start(pred[8,128]{1,0:T(8,128)(4,1)} %get-tuple-element.22) | copy-start | bytes 3076
  117.3 0.6 copy-start.11
  139.6 5.1 %copy-start.9 = (bf16[4,8,4,128]{3,1,2,0:T(8,128)(2,1)S(1)}, bf16[4,8,4,128]{3,1,2,0:T(8,128)(2,1)}, u32[]{:S(2)}) copy-start(bf16[4,8,4,128]{3,1,2,0:T(8,128)(2,1)} %fusion.53) | copy-start | bytes 98308

commit v3 on v2

--- a/solution.py
+++ b/solution.py
@@ -123,82 +123,160 @@
     )(x)
 
 
-def peak_kernel(n, x_ref, o_ref, landed, send_sem, recv_sem):
+def merge_kernel(
+    n, per, x_ref, lse_ref, o_ref, sent, landed, logs, whole, send_one, recv_one, send_log, recv_log, send_two, recv_two
+):
     me = lax.axis_index("seq")
     barrier = greet(n, me)
+    blocks = x_ref.shape[1] // LANES
+    for j in range(blocks):
+        sent[j] = x_ref[:, j * LANES : (j + 1) * LANES]
+    for j in range(blocks, n * per):
+        sent[j] = jnp.zeros(sent.shape[1:], sent.dtype)
     pl.semaphore_wait(barrier, n - 1)
-    out = []
-    for off in range(1, n):
-        out.append(remote(n, me, off, x_ref, landed.at[off - 1], send_sem, recv_sem))
+    out, told = [], []
+    for off in range(1, n):
+        told.append(remote(n, me, off, lse_ref, logs.at[off - 1], send_log, recv_log))
+        told[-1].start()
+        part = pl.ds(lax.rem(me + off, n) * per, per)
+        out.append(remote(n, me, off, sent.at[part], landed.at[off - 1], send_one, recv_one))
         out[-1].start()
-    top = x_ref[...]
+    for copy in told:
+        copy.wait_recv()
+    lse = [lse_ref[...]] + [logs[off - 1] for off in range(1, n)]
+    top = functools.reduce(jnp.maximum, lse)
+    weights = [jnp.exp(one - top) for one in lse]
+    scale = 1.0 / functools.reduce(jnp.add, weights)
+    lane = lax.broadcasted_iota(jnp.int32, top.shape, 1)
+
+    def column(weight, p):
+        here = lane == me * per + p
+        return jnp.sum(jnp.where(here, weight * scale, 0.0), axis=1, keepdims=True)
+
+    total = [column(weights[0], p) * sent[me * per + p].astype(jnp.float32) for p in range(per)]
     for off in range(1, n):
         out[off - 1].wait_recv()
-        top = jnp.maximum(top, landed[off - 1])
-    o_ref[...] = top
-    for copy in out:
+        for p in range(per):
+            total[p] = total[p] + column(weights[off], p) * landed[off - 1, p].astype(jnp.float32)
+    for p in range(per):
+        whole[me * per + p] = total[p].astype(whole.dtype)
+    mine = pl.ds(me * per, per)
+    back = []
+    for off in range(1, n):
+        back.append(remote(n, me, off, whole.at[mine], whole.at[mine], send_two, recv_two))
+        back[-1].start()
+    for copy in told + out:
         copy.wait_send()
-
-
-def peak_over(x, n, ident):
-    tile = 8 * LANES
-    padded = -(-x.size // tile) * tile
-    flat = jnp.pad(x.reshape(-1), (0, padded - x.size)).reshape(-1, LANES)
+    for copy in back:
+        copy.wait_recv()
+    for j in range(blocks):
+        o_ref[:, j * LANES : (j + 1) * LANES] = whole[j]
+    for copy in back:
+        copy.wait_send()
+
+
+def merge_over(values, lse, n, ident):
+    rows, columns = values.shape
+    per = -(-(columns // LANES) // n)
     vmem = pl.BlockSpec(memory_space=pltpu.VMEM)
     dma = pltpu.SemaphoreType.DMA((n - 1,))
-    top = pl.pallas_call(
-        functools.partial(peak_kernel, n),
-        out_shape=jax.ShapeDtypeStruct(flat.shape, jnp.float32),
-        in_specs=[vmem],
+    return pl.pallas_call(
+        functools.partial(merge_kernel, n, per),
+        out_shape=jax.ShapeDtypeStruct(values.shape, jnp.bfloat16),
+        in_specs=[vmem, vmem],
         out_specs=vmem,
-        scratch_shapes=[pltpu.VMEM((n - 1,) + flat.shape, jnp.float32), dma, dma],
+        scratch_shapes=[
+            pltpu.VMEM((n * per, rows, LANES), jnp.bfloat16),
+            pltpu.VMEM((n - 1, per, rows, LANES), jnp.bfloat16),
+            pltpu.VMEM((n - 1, rows, LANES), jnp.float32),
+            pltpu.VMEM((n * per, rows, LANES), jnp.bfloat16),
+        ]
+        + [dma] * 6,
         compiler_params=pltpu.CompilerParams(
             collective_id=ident, has_side_effects=True, vmem_limit_bytes=16 * 2**20
         ),
-    )(flat)
-    return top.reshape(-1)[: x.size].reshape(x.shape)
-
-
-def attend(query, keys, values, new_keys, new_values, live, first, shards, ident):
+    )(values, lse)
+
+
+def attend_kernel(steps, group, len_ref, q_ref, k_ref, v_ref, nk_ref, nv_ref, o_ref, lse_ref):
+    me = lax.axis_index("seq")
+    heads, padded, width = q_ref.shape[1:]
+    count = k_ref.shape[1]
+    fresh_count = nk_ref.shape[2]
+    scale = width ** (-0.5)
+    length = len_ref[pl.program_id(0)]
+    place = me * count + lax.broadcasted_iota(jnp.int32, (padded, count), 1)
+    live = place < length
+    row = lax.broadcasted_iota(jnp.int32, (padded, fresh_count), 0)
+    slot = lax.broadcasted_iota(jnp.int32, (padded, fresh_count), 1)
+    fresh_live = (slot * group <= row) & (slot < steps) & (me == 0)
+    across = (((1,), (1,)), ((), ()))
+    for k in range(heads):
+        part = slice(k * width, (k + 1) * width)
+        q = q_ref[0, k]
+        cached = lax.dot_general(q, k_ref[0, :, part], across, preferred_element_type=jnp.float32)
+        fresh = lax.dot_general(q, nk_ref[0, k], across, preferred_element_type=jnp.float32)
+        cached = jnp.where(live, cached * scale, NEGATIVE)
+        fresh = jnp.where(fresh_live, fresh * scale, NEGATIVE)
+        peak = jnp.maximum(
+            jnp.max(cached, axis=1, keepdims=True), jnp.max(fresh, axis=1, keepdims=True)
+        )
+        weight = jnp.where(live, jnp.exp(cached - peak), 0.0)
+        weight_fresh = jnp.where(fresh_live, jnp.exp(fresh - peak), 0.0)
+        total = jnp.sum(weight, axis=1, keepdims=True) + jnp.sum(
+            weight_fresh, axis=1, keepdims=True
+        )
+        summed = jnp.dot(
+            weight.astype(jnp.bfloat16), v_ref[0, :, part], preferred_element_type=jnp.float32
+        ) + jnp.dot(
+            weight_fresh.astype(jnp.bfloat16), nv_ref[0, k], preferred_element_type=jnp.float32
+        )
+        safe = jnp.maximum(total, 0.5)
+        o_ref[0, k] = (summed / safe).astype(o_ref.dtype)
+        log = jnp.where(total > 0.5, peak + jnp.log(safe), NEGATIVE)
+        lse_ref[0, k] = jnp.broadcast_to(log, (padded, width))
+
+
+def attend(query, keys, values, new_keys, new_values, lengths, shards, ident):
     batch, steps, heads, group, width = query.shape
     count = keys.shape[1]
-    scale = width ** (-0.5)
-    key_four = keys.reshape(batch, count, heads, width)
-    value_four = values.reshape(batch, count, heads, width)
-    cached = (
-        jnp.einsum("bskgd,btkd->bksgt", query, key_four, preferred_element_type=jnp.float32) * scale
-    )
-    fresh = (
-        jnp.einsum("bskgd,bukd->bksgu", query, new_keys, preferred_element_type=jnp.float32) * scale
-    )
-    order = jnp.arange(steps)
-    live_mask = live[:, None, None, None, :]
-    fresh_mask = ((order[None, :] <= order[:, None]) & first)[None, None, :, None, :]
-    cached = jnp.where(live_mask, cached, NEGATIVE)
-    fresh = jnp.where(fresh_mask, fresh, NEGATIVE)
-    peak = peak_over(jnp.maximum(cached.max(-1), fresh.max(-1)), shards, ident)
-    weight_cached = jnp.where(live_mask, jnp.exp(cached - peak[..., None]), 0.0)
-    weight_fresh = jnp.where(fresh_mask, jnp.exp(fresh - peak[..., None]), 0.0)
-    total = weight_cached.sum(-1) + weight_fresh.sum(-1)
-    summed = jnp.einsum(
-        "bksgt,btkd->bksgd",
-        weight_cached.astype(jnp.bfloat16),
-        value_four,
-        preferred_element_type=jnp.float32,
-    ) + jnp.einsum(
-        "bksgu,bukd->bksgd",
-        weight_fresh.astype(jnp.bfloat16),
-        new_values,
-        preferred_element_type=jnp.float32,
-    )
-    rows, count = steps * batch, heads * group
-    totals = total.transpose(2, 0, 1, 3).reshape(rows, count)
-    totals = jnp.pad(totals, ((0, 0), (0, -count % LANES)))
-    values = summed.transpose(2, 0, 1, 3, 4).reshape(rows, count * width)
-    both = sum_over(jnp.concatenate([values, totals], axis=1), shards, ident + 1)
-    out = both[:, : count * width].reshape(rows, count, width)
-    total = both[:, count * width : count * width + count]
-    return (out / total[:, :, None]).astype(jnp.bfloat16).reshape(rows, count * width)
+    used = steps * group
+    padded = -(-used // 16) * 16
+    quest = query.transpose(0, 2, 1, 3, 4).reshape(batch, heads, used, width)
+    quest = jnp.pad(quest, ((0, 0), (0, 0), (0, padded - used), (0, 0)))
+
+    def slots(new):
+        return jnp.pad(new.transpose(0, 2, 1, 3), ((0, 0), (0, 0), (0, -steps % 16), (0, 0)))
+
+    new_keys, new_values = slots(new_keys), slots(new_values)
+
+    def spec(shape):
+        return pl.BlockSpec((1,) + shape, lambda b: (b,) + (0,) * len(shape))
+
+    cache = spec((count, heads * width))
+    fresh = spec(new_keys.shape[1:])
+    rows_spec = spec((heads, padded, width))
+    out, lse = pl.pallas_call(
+        functools.partial(attend_kernel, steps, group),
+        grid=(batch,),
+        out_shape=(
+            jax.ShapeDtypeStruct(quest.shape, jnp.bfloat16),
+            jax.ShapeDtypeStruct(quest.shape, jnp.float32),
+        ),
+        in_specs=[
+            pl.BlockSpec(memory_space=pltpu.SMEM), rows_spec, cache, cache, fresh, fresh
+        ],
+        out_specs=(rows_spec, rows_spec),
+        compiler_params=pltpu.CompilerParams(vmem_limit_bytes=16 * 2**20),
+    )(lengths, quest, keys, values, new_keys, new_values)
+
+    def by_row(x):
+        x = x[:, :, :used].reshape(batch, heads, steps, group, -1).transpose(2, 0, 1, 3, 4)
+        return x.reshape(steps * batch, -1)
+
+    logs = by_row(lse[..., :1])
+    logs = jnp.pad(logs, ((0, 0), (0, LANES - logs.shape[1])))
+    return merge_over(by_row(out), logs, shards, ident)
 
 
 def body(
@@ -229,10 +307,6 @@
     audio_q = AHQ * AHD
     audio_kv = AHK * AHD
 
-    def live_of(cache, lengths):
-        count = cache.shape[1]
-        return (index * count + jnp.arange(count))[None, :] < lengths[:, None]
-
     def by_batch(heads):
         return heads.reshape((steps, batch) + heads.shape[1:]).swapaxes(0, 1)
 
@@ -261,8 +335,7 @@
         text_values,
         by_batch(key),
         by_batch(value),
-        live_of(text_keys, text_len),
-        index == 0,
+        text_len,
         shards,
         1,
     )
@@ -298,8 +371,7 @@
         audio_values,
         by_batch(key),
         by_batch(value),
-        live_of(audio_keys, audio_len),
-        index == 0,
+        audio_len,
         shards,
         5,
     )

time: 159 us -> 137 us (0.86)
  Pallas kernels: 85.9 us -> 100 us
  local copies, waits for them, and re-layouts: 30.4 us -> 17 us
  matrix products: 23.2 us -> 9.81 us
  other arithmetic: 17.1 us -> 8.58 us
    pallas_call x2 -> x4, Pallas kernels: 13.5 us -> 53.4 us  [the longest x2 33.9 us: merge_over(): pl.pallas_call(functools.partial(merge_kernel, n, per), out_shape=jax.Sha...]
    pallas_call x5 -> x3, Pallas kernels: 72.4 us -> 46.6 us  [sum_over(): pl.pallas_call(functools.partial(sum_kernel, n, per), out_shape=jax.Shape...]
    dot_general x8 -> x0, matrix products: 15.7 us -> none  [the longest x2 5.67 us: attend(): jnp.einsum('bskgd,btkd->bksgt', query, key_four, preferred_element_type=j...]
    reshape x10 -> x7, local copies, waits for them, and re-layouts: 10.9 us -> 1.94 us  [the longest x4 1.78 us: by_row(): return x.reshape(steps * batch, -1)]
    reduce_sum x3 -> x0, other arithmetic: 3.69 us -> none  [attend(): total = weight_cached.sum(-1) + weight_fresh.sum(-1)]
    slice x4, local copies, waits for them, and re-layouts: 0.04 us -> 2.86 us  [by_row(): x[:, :, :used].reshape(batch, heads, steps, group, -1)]
    dot_general x1, matrix products: 0.92 us -> 3.22 us  [body(): spoken = jnp.dot(normed, talker_qkv, preferred_element_type=jnp.float32)]
    convert_element_type x1 -> x0, other arithmetic: 2.01 us -> none  [attend(): weight_fresh.astype(jnp.bfloat16)]
where the time goes in v3:
time: 137 us
  Pallas kernels  100 us (73%)
  local copies, waits for them, and re-layouts  17 us (12%)
  matrix products  9.81 us (7%)
  other arithmetic  8.58 us (6%)
    pallas_call x3, Pallas kernels, sum_over(): pl.pallas_call(functools.partial(sum_kernel, n, per), out_shape=jax.Shape...  46.6 us
    pallas_call x2, Pallas kernels, merge_over(): pl.pallas_call(functools.partial(merge_kernel, n, per), out_shape=jax.Sha...  33.9 us
    pallas_call x2, Pallas kernels, attend(): pl.pallas_call(functools.partial(attend_kernel, steps, group), grid=(batc...  19.6 us
    dot_general x1, matrix products, body(): spoken = jnp.dot(normed, talker_qkv, preferred_element_type=jnp.float32)  3.22 us
    dot_general x1, matrix products, body(): jnp.dot(mine, thinker_qkv, preferred_element_type=jnp.float32)  3.06 us
    another operation x2, other arithmetic  2.91 us
    slice x4, local copies, waits for them, and re-layouts, by_row(): x[:, :, :used].reshape(batch, heads, steps, group, -1)  2.86 us

profile of v3, /device:TPU:0, one launch (start us, length us, event | category | flops | bytes accessed | tf_op | source)
XLA Modules:
  0.0 136.6 jit_solution(3753305388028588013)
XLA Ops:
  0.7 0.9 eq.15
  1.6 0.8 dynamic-slice
  3.9 1.1 fusion.2
  5.9 1.0 convert_bitcast_fusion
  6.8 3.1 %fusion.15.x_ref = f32[32,4608]{1,0:T(8,128)S(1)} fusion(bf16[448,4608]{1,0:T(8,128)(2,1)} %param.20, f32[32,3584]{1,0:T(8,128)S(1)} %convert_bitcast_fusion, s32[]{:T(128)S(6)} %select_n.4, f32[448]{0:T(512)S(1)} %dynamic-slice), kind=kOutput, calls=%fused_computation.36 | convolution fusion | flops 132149248 | bytes 4786180 | tf_op jit(solution)/shard_map/dot_general | solution.py:326
  9.9 18.4 %shard_map.185 = f32[32,4608]{1,0:T(8,128)S(1)} custom-call(f32[32,4608]{1,0:T(8,128)S(1)} %fusion.15.x_ref), custom_call_target="tpu_custom_call" | custom-call | tf_op jit(solution)/shard_map/pallas_call | solution.py:106
  28.5 0.8 slice.78
  29.3 1.9 %reshape.224 = f32[32,28,128]{2,1,0:T(8,128)} reshape(f32[32,3584]{1,0:T(8,128)} %slice.78) | data formatting | bytes 917504 | tf_op jit(solution)/shard_map/reshape | solution.py:329
  31.2 1.6 %subtract_convert_fusion = (bf16[32,28,64]{2,1,0:T(8,128)(2,1)S(1)}, bf16[32,28,64]{2,1,0:T(8,128)(2,1)S(1)}) fusion(f32[32,28,128]{2,1,0:T(8,128)} %reshape.224, f32[32,64]{1,0:T(8,128)S(1)} %get-tuple-element.26, f32[32,64]{1,0:T(8,128)S(1)} %get-tuple-element.27), kind=kLoop, calls=%fused_computation.7 | loop fusion | flops 458752 | bytes 704512 | tf_op jit(solution)/shard_map/convert.18
  33.7 9.8 %shard_map.186 = (bf16[8,4,32,128]{3,2,1,0:T(8,128)(2,1)S(1)}, f32[8,4,32,128]{3,2,1,0:T(8,128)S(1)}) custom-call(s32[8]{0:T(128)S(1)} %copy-done.7, bf16[8,4,32,128]{3,2,1,0:T(8,128)(2,1)S(1)} %pad.29.q_ref, bf16[8,128,512]{2,1,0:T(8,128)(2,1)S(1)} %copy-done.1, bf16[8,128,512]{2,1,0:T(8,128)(2,1)S(1)} %copy-done.2, ...), custom_call_target="tpu_custom_call" | custom-call | tf_op jit(solution)/shard_map/pallas_call | solution.py:259
  43.5 0.8 copy-done.5
  44.5 1.3 copy.35
  46.6 0.9 reshape.241
  47.6 20.4 %shard_map.187 = bf16[32,3584]{1,0:T(8,128)(2,1)S(1)} custom-call(bf16[32,3584]{1,0:T(8,128)(2,1)S(1)} %bitcast.74, f32[32,128]{1,0:T(8,128)S(1)} %pad.32.lse_ref), custom_call_target="tpu_custom_call" | custom-call | tf_op jit(solution)/shard_map/pallas_call | solution.py:183
  68.7 15.8 %shard_map.188 = f32[32,3584]{1,0:T(8,128)S(1)} custom-call(f32[32,3584]{1,0:T(8,128)S(1)} %fusion.22.x_ref), custom_call_target="tpu_custom_call" | custom-call | tf_op jit(solution)/shard_map/pallas_call | solution.py:106
  85.4 12.4 %shard_map.189 = f32[32,896]{1,0:T(8,128)S(1)} custom-call(f32[32,896]{1,0:T(8,128)S(1)} %convolution_add_fusion.x_ref), custom_call_target="tpu_custom_call" | custom-call | tf_op jit(solution)/shard_map/pallas_call | solution.py:106
  97.9 3.2 %fusion.8 = f32[32,2560]{1,0:T(8,128)S(1)} fusion(bf16[896,2560]{1,0:T(8,128)(2,1)} %param.25, f32[32,896]{1,0:T(8,128)S(1)} %shard_map.189, f32[896]{0:T(1024)S(1)} %copy-done.13, f32[32]{0:T(128)S(1)} %add_rsqrt_fusion.1), kind=kOutput, calls=%fused_computation.29 | convolution fusion | flops 146886656 | bytes 5033600 | tf_op jit(solution)/shard_map/dot_general | solution.py:362
  102.5 1.5 %reshape.234 = f32[32,4,128]{2,1,0:T(4,128)} reshape(f32[32,512]{1,0:T(8,128)} %slice.88) | data formatting | bytes 131072 | tf_op jit(solution)/shard_map/reshape | solution.py:365
  104.7 1.3 subtract_convert_fusion.1
  106.0 1.0 fusion.28
  109.0 9.7 %shard_map.190 = (bf16[8,4,16,128]{3,2,1,0:T(8,128)(2,1)S(1)}, f32[8,4,16,128]{3,2,1,0:T(8,128)S(1)}) custom-call(s32[8]{0:T(128)S(1)} %copy-done.8, bf16[8,4,16,128]{3,2,1,0:T(8,128)(2,1)S(1)} %pad.33.q_ref, bf16[8,128,512]{2,1,0:T(8,128)(2,1)S(1)} %copy-done.3, bf16[8,128,512]{2,1,0:T(8,128)(2,1)S(1)} %copy-done.4, ...), custom_call_target="tpu_custom_call" | custom-call | tf_op jit(solution)/shard_map/pallas_call | solution.py:259
  119.5 1.3 copy.49
  121.0 13.5 %shard_map.191 = bf16[32,1536]{1,0:T(8,128)(2,1)S(1)} custom-call(bf16[32,1536]{1,0:T(8,128)(2,1)S(1)} %bitcast.76, f32[32,128]{1,0:T(8,128)S(1)} %pad.36.lse_ref), custom_call_target="tpu_custom_call" | custom-call | tf_op jit(solution)/shard_map/pallas_call | solution.py:183
  134.5 2.1 %fusion.1 = bf16[4,8,112]{2,1,0:T(8,128)(2,1)} fusion(bf16[32,1536]{1,0:T(8,128)(2,1)S(1)} %shard_map.191, bf16[1536,896]{1,0:T(8,128)(2,1)} %param.26, s32[]{:T(128)S(6)} %select_n.10, f32[32,896]{1,0:T(8,128)S(1)} %shard_map.189), kind=kOutput, calls=%fused_computation.3 | convolution fusion | flops 11017216 | bytes 514048 | tf_op jit(solution)/shard_map/dot_general | solution.py:379
  (88 shorter events, 10.8 us)
Async XLA Ops:
  0.6 67.3 %copy-start = (bf16[448,3584]{1,0:T(8,128)(2,1)S(1)}, bf16[448,3584]{1,0:T(8,128)(2,1)}, u32[]{:S(2)}) copy-start(bf16[448,3584]{1,0:T(8,128)(2,1)} %param.21) | copy-start | bytes 9633796
  29.3 4.3 %copy-start.7 = (s32[8]{0:T(128)S(1)}, s32[8]{0:T(128)}, u32[]{:S(2)}) copy-start(s32[8]{0:T(128)} %len_ref.2) | copy-start | bytes 100
  31.2 2.4 %copy-start.1 = (bf16[8,128,512]{2,1,0:T(8,128)(2,1)S(1)}, bf16[8,128,512]{2,1,0:T(8,128)(2,1)}, u32[]{:S(2)}) copy-start(bf16[8,128,512]{2,1,0:T(8,128)(2,1)} %k_ref.2) | copy-start | bytes 3145732
  31.2 2.4 %copy-start.2 = (bf16[8,128,512]{2,1,0:T(8,128)(2,1)S(1)}, bf16[8,128,512]{2,1,0:T(8,128)(2,1)}, u32[]{:S(2)}) copy-start(bf16[8,128,512]{2,1,0:T(8,128)(2,1)} %v_ref.2) | copy-start | bytes 3145732
  43.5 0.8 copy-start.5
  47.5 37.0 %copy-start.9 = (bf16[4,8,3584]{2,1,0:T(8,128)(2,1)S(1)}, bf16[4,8,3584]{2,1,0:T(8,128)(2,1)}, u32[]{:S(2)}) copy-start(bf16[4,8,3584]{2,1,0:T(8,128)(2,1)} %param.18) | copy-start | bytes 688132
  47.5 37.1 %copy-start.11 = (bf16[448,896]{1,0:T(8,128)(2,1)S(1)}, bf16[448,896]{1,0:T(8,128)(2,1)}, u32[]{:S(2)}) copy-start(bf16[448,896]{1,0:T(8,128)(2,1)} %param.22) | copy-start | bytes 2408452
  68.0 16.9 %copy-start.10 = (bf16[1056,896]{1,0:T(8,128)(2,1)S(1)}, bf16[1056,896]{1,0:T(8,128)(2,1)}, u32[]{:S(2)}) copy-start(bf16[1056,896]{1,0:T(8,128)(2,1)} %param.23) | copy-start | bytes 5677060
  68.7 29.2 %copy-start.13 = (f32[896]{0:T(1024)S(1)}, f32[896]{0:T(1024)}, u32[]{:S(2)}) copy-start(f32[896]{0:T(1024)} %param.24) | copy-start | bytes 10756
  84.6 16.6 %copy-start.12 = (bf16[32,3584]{1,0:T(8,128)(2,1)}, bf16[32,3584]{1,0:T(8,128)(2,1)S(1)}, u32[]{:S(2)}) copy-start(bf16[32,3584]{1,0:T(8,128)(2,1)S(1)} %add_convert_fusion.1) | copy-start | bytes 688132
  101.2 7.8 %copy-start.8 = (s32[8]{0:T(128)S(1)}, s32[8]{0:T(128)}, u32[]{:S(2)}) copy-start(s32[8]{0:T(128)} %len_ref.3) | copy-start | bytes 100
  104.7 4.3 %copy-start.3 = (bf16[8,128,512]{2,1,0:T(8,128)(2,1)S(1)}, bf16[8,128,512]{2,1,0:T(8,128)(2,1)}, u32[]{:S(2)}) copy-start(bf16[8,128,512]{2,1,0:T(8,128)(2,1)} %k_ref.3) | copy-start | bytes 3145732
  104.7 4.3 %copy-start.4 = (bf16[8,128,512]{2,1,0:T(8,128)(2,1)S(1)}, bf16[8,128,512]{2,1,0:T(8,128)(2,1)}, u32[]{:S(2)}) copy-start(bf16[8,128,512]{2,1,0:T(8,128)(2,1)} %v_ref.3) | copy-start | bytes 3145732
  118.8 0.7 copy-start.6

commit v4 on v3

--- a/solution.py
+++ b/solution.py
@@ -1,4 +1,5 @@
 import functools
+import math
 
 import jax
 import jax.numpy as jnp
@@ -204,18 +205,18 @@
     count = k_ref.shape[1]
     fresh_count = nk_ref.shape[2]
     scale = width ** (-0.5)
-    length = len_ref[pl.program_id(0)]
+    fold = q_ref.shape[0]
     place = me * count + lax.broadcasted_iota(jnp.int32, (padded, count), 1)
-    live = place < length
     row = lax.broadcasted_iota(jnp.int32, (padded, fresh_count), 0)
     slot = lax.broadcasted_iota(jnp.int32, (padded, fresh_count), 1)
     fresh_live = (slot * group <= row) & (slot < steps) & (me == 0)
     across = (((1,), (1,)), ((), ()))
-    for k in range(heads):
+    for c, k in [(c, k) for c in range(fold) for k in range(heads)]:
+        live = place < len_ref[pl.program_id(0) * fold + c]
         part = slice(k * width, (k + 1) * width)
-        q = q_ref[0, k]
-        cached = lax.dot_general(q, k_ref[0, :, part], across, preferred_element_type=jnp.float32)
-        fresh = lax.dot_general(q, nk_ref[0, k], across, preferred_element_type=jnp.float32)
+        q = q_ref[c, k]
+        cached = lax.dot_general(q, k_ref[c, :, part], across, preferred_element_type=jnp.float32)
+        fresh = lax.dot_general(q, nk_ref[c, k], across, preferred_element_type=jnp.float32)
         cached = jnp.where(live, cached * scale, NEGATIVE)
         fresh = jnp.where(fresh_live, fresh * scale, NEGATIVE)
         peak = jnp.maximum(
@@ -227,19 +228,20 @@
             weight_fresh, axis=1, keepdims=True
         )
         summed = jnp.dot(
-            weight.astype(jnp.bfloat16), v_ref[0, :, part], preferred_element_type=jnp.float32
+            weight.astype(jnp.bfloat16), v_ref[c, :, part], preferred_element_type=jnp.float32
         ) + jnp.dot(
-            weight_fresh.astype(jnp.bfloat16), nv_ref[0, k], preferred_element_type=jnp.float32
+            weight_fresh.astype(jnp.bfloat16), nv_ref[c, k], preferred_element_type=jnp.float32
         )
         safe = jnp.maximum(total, 0.5)
-        o_ref[0, k] = (summed / safe).astype(o_ref.dtype)
+        o_ref[c, k] = (summed / safe).astype(o_ref.dtype)
         log = jnp.where(total > 0.5, peak + jnp.log(safe), NEGATIVE)
-        lse_ref[0, k] = jnp.broadcast_to(log, (padded, width))
+        lse_ref[c, k] = jnp.broadcast_to(log, (padded, width))
 
 
 def attend(query, keys, values, new_keys, new_values, lengths, shards, ident):
     batch, steps, heads, group, width = query.shape
     count = keys.shape[1]
+    fold = math.gcd(batch, 4)
     used = steps * group
     padded = -(-used // 16) * 16
     quest = query.transpose(0, 2, 1, 3, 4).reshape(batch, heads, used, width)
@@ -251,14 +253,14 @@
     new_keys, new_values = slots(new_keys), slots(new_values)
 
     def spec(shape):
-        return pl.BlockSpec((1,) + shape, lambda b: (b,) + (0,) * len(shape))
+        return pl.BlockSpec((fold,) + shape, lambda b: (b,) + (0,) * len(shape))
 
     cache = spec((count, heads * width))
     fresh = spec(new_keys.shape[1:])
     rows_spec = spec((heads, padded, width))
     out, lse = pl.pallas_call(
         functools.partial(attend_kernel, steps, group),
-        grid=(batch,),
+        grid=(batch // fold,),
         out_shape=(
             jax.ShapeDtypeStruct(quest.shape, jnp.bfloat16),
             jax.ShapeDtypeStruct(quest.shape, jnp.float32),

time: 137 us -> 136 us (level)
  Pallas kernels: 100 us -> 98.6 us
    pallas_call x2, Pallas kernels: 19.6 us -> 18.1 us  [attend(): pl.pallas_call(functools.partial(attend_kernel, steps, group), grid=(batc...]
where the time goes in v4:
time: 136 us; the launch traced here: 135 us
  Pallas kernels  98.6 us (72%)
  local copies, waits for them, and re-layouts  17 us (12%)
  matrix products  9.81 us (7%)
  other arithmetic  8.58 us (6%)
    pallas_call x3, Pallas kernels, sum_over(): pl.pallas_call(functools.partial(sum_kernel, n, per), out_shape=jax.Shape...  46.6 us
    pallas_call x2, Pallas kernels, merge_over(): pl.pallas_call(functools.partial(merge_kernel, n, per), out_shape=jax.Sha...  33.9 us
    pallas_call x2, Pallas kernels, attend(): pl.pallas_call(functools.partial(attend_kernel, steps, group), grid=(batc...  18.1 us
    dot_general x1, matrix products, body(): spoken = jnp.dot(normed, talker_qkv, preferred_element_type=jnp.float32)  3.22 us
    dot_general x1, matrix products, body(): jnp.dot(mine, thinker_qkv, preferred_element_type=jnp.float32)  3.06 us
    another operation x2, other arithmetic  2.91 us
    slice x4, local copies, waits for them, and re-layouts, by_row(): x[:, :, :used].reshape(batch, heads, steps, group, -1)  2.86 us

profile of v4, /device:TPU:0, one launch (start us, length us, event | category | flops | bytes accessed | tf_op | source)
XLA Modules:
  0.0 135.2 jit_solution(2355112934751710692)
XLA Ops:
  0.7 0.9 eq.15
  1.6 0.8 dynamic-slice
  3.9 1.1 fusion.2
  5.9 1.0 convert_bitcast_fusion
  6.8 3.1 %fusion.15.x_ref = f32[32,4608]{1,0:T(8,128)S(1)} fusion(bf16[448,4608]{1,0:T(8,128)(2,1)} %param.20, f32[32,3584]{1,0:T(8,128)S(1)} %convert_bitcast_fusion, s32[]{:T(128)S(6)} %select_n.4, f32[448]{0:T(512)S(1)} %dynamic-slice), kind=kOutput, calls=%fused_computation.36 | convolution fusion | flops 132149248 | bytes 4786180 | tf_op jit(solution)/shard_map/dot_general | solution.py:328
  9.9 18.4 %shard_map.185 = f32[32,4608]{1,0:T(8,128)S(1)} custom-call(f32[32,4608]{1,0:T(8,128)S(1)} %fusion.15.x_ref), custom_call_target="tpu_custom_call" | custom-call | tf_op jit(solution)/shard_map/pallas_call | solution.py:107
  28.5 0.8 slice.78
  29.3 1.9 %reshape.224 = f32[32,28,128]{2,1,0:T(8,128)} reshape(f32[32,3584]{1,0:T(8,128)} %slice.78) | data formatting | bytes 917504 | tf_op jit(solution)/shard_map/reshape | solution.py:331
  31.2 1.6 %subtract_convert_fusion = (bf16[32,28,64]{2,1,0:T(8,128)(2,1)S(1)}, bf16[32,28,64]{2,1,0:T(8,128)(2,1)S(1)}) fusion(f32[32,28,128]{2,1,0:T(8,128)} %reshape.224, f32[32,64]{1,0:T(8,128)S(1)} %get-tuple-element.26, f32[32,64]{1,0:T(8,128)S(1)} %get-tuple-element.27), kind=kLoop, calls=%fused_computation.7 | loop fusion | flops 458752 | bytes 704512 | tf_op jit(solution)/shard_map/convert.18
  33.7 9.1 %shard_map.186 = (bf16[8,4,32,128]{3,2,1,0:T(8,128)(2,1)S(1)}, f32[8,4,32,128]{3,2,1,0:T(8,128)S(1)}) custom-call(s32[8]{0:T(128)S(1)} %copy-done.7, bf16[8,4,32,128]{3,2,1,0:T(8,128)(2,1)S(1)} %pad.29.q_ref, bf16[8,128,512]{2,1,0:T(8,128)(2,1)S(1)} %copy-done.1, bf16[8,128,512]{2,1,0:T(8,128)(2,1)S(1)} %copy-done.2, ...), custom_call_target="tpu_custom_call" | custom-call | tf_op jit(solution)/shard_map/pallas_call | solution.py:261
  42.8 0.8 copy-done.5
  43.8 1.3 copy.35
  45.9 0.9 reshape.241
  46.8 20.4 %shard_map.187 = bf16[32,3584]{1,0:T(8,128)(2,1)S(1)} custom-call(bf16[32,3584]{1,0:T(8,128)(2,1)S(1)} %bitcast.74, f32[32,128]{1,0:T(8,128)S(1)} %pad.32.lse_ref), custom_call_target="tpu_custom_call" | custom-call | tf_op jit(solution)/shard_map/pallas_call | solution.py:184
  68.0 15.8 %shard_map.188 = f32[32,3584]{1,0:T(8,128)S(1)} custom-call(f32[32,3584]{1,0:T(8,128)S(1)} %fusion.22.x_ref), custom_call_target="tpu_custom_call" | custom-call | tf_op jit(solution)/shard_map/pallas_call | solution.py:107
  84.7 12.4 %shard_map.189 = f32[32,896]{1,0:T(8,128)S(1)} custom-call(f32[32,896]{1,0:T(8,128)S(1)} %convolution_add_fusion.x_ref), custom_call_target="tpu_custom_call" | custom-call | tf_op jit(solution)/shard_map/pallas_call | solution.py:107
  97.2 3.2 %fusion.8 = f32[32,2560]{1,0:T(8,128)S(1)} fusion(bf16[896,2560]{1,0:T(8,128)(2,1)} %param.25, f32[32,896]{1,0:T(8,128)S(1)} %shard_map.189, f32[896]{0:T(1024)S(1)} %copy-done.13, f32[32]{0:T(128)S(1)} %add_rsqrt_fusion.1), kind=kOutput, calls=%fused_computation.29 | convolution fusion | flops 146886656 | bytes 5033600 | tf_op jit(solution)/shard_map/dot_general | solution.py:364
  101.7 1.5 %reshape.234 = f32[32,4,128]{2,1,0:T(4,128)} reshape(f32[32,512]{1,0:T(8,128)} %slice.88) | data formatting | bytes 131072 | tf_op jit(solution)/shard_map/reshape | solution.py:367
  104.0 1.3 subtract_convert_fusion.1
  105.3 1.0 fusion.28
  108.3 9.0 %shard_map.190 = (bf16[8,4,16,128]{3,2,1,0:T(8,128)(2,1)S(1)}, f32[8,4,16,128]{3,2,1,0:T(8,128)S(1)}) custom-call(s32[8]{0:T(128)S(1)} %copy-done.8, bf16[8,4,16,128]{3,2,1,0:T(8,128)(2,1)S(1)} %pad.33.q_ref, bf16[8,128,512]{2,1,0:T(8,128)(2,1)S(1)} %copy-done.3, bf16[8,128,512]{2,1,0:T(8,128)(2,1)S(1)} %copy-done.4, ...), custom_call_target="tpu_custom_call" | custom-call | tf_op jit(solution)/shard_map/pallas_call | solution.py:261
  118.1 1.3 copy.49
  119.6 13.5 %shard_map.191 = bf16[32,1536]{1,0:T(8,128)(2,1)S(1)} custom-call(bf16[32,1536]{1,0:T(8,128)(2,1)S(1)} %bitcast.76, f32[32,128]{1,0:T(8,128)S(1)} %pad.36.lse_ref), custom_call_target="tpu_custom_call" | custom-call | tf_op jit(solution)/shard_map/pallas_call | solution.py:184
  133.1 2.1 %fusion.1 = bf16[4,8,112]{2,1,0:T(8,128)(2,1)} fusion(bf16[32,1536]{1,0:T(8,128)(2,1)S(1)} %shard_map.191, bf16[1536,896]{1,0:T(8,128)(2,1)} %param.26, s32[]{:T(128)S(6)} %select_n.10, f32[32,896]{1,0:T(8,128)S(1)} %shard_map.189), kind=kOutput, calls=%fused_computation.3 | convolution fusion | flops 11017216 | bytes 514048 | tf_op jit(solution)/shard_map/dot_general | solution.py:381
  (88 shorter events, 10.8 us)
Async XLA Ops:
  0.6 66.6 %copy-start = (bf16[448,3584]{1,0:T(8,128)(2,1)S(1)}, bf16[448,3584]{1,0:T(8,128)(2,1)}, u32[]{:S(2)}) copy-start(bf16[448,3584]{1,0:T(8,128)(2,1)} %param.21) | copy-start | bytes 9633796
  29.3 4.3 %copy-start.7 = (s32[8]{0:T(128)S(1)}, s32[8]{0:T(128)}, u32[]{:S(2)}) copy-start(s32[8]{0:T(128)} %len_ref.2) | copy-start | bytes 100
  31.2 2.4 %copy-start.1 = (bf16[8,128,512]{2,1,0:T(8,128)(2,1)S(1)}, bf16[8,128,512]{2,1,0:T(8,128)(2,1)}, u32[]{:S(2)}) copy-start(bf16[8,128,512]{2,1,0:T(8,128)(2,1)} %k_ref.2) | copy-start | bytes 3145732
  31.2 2.4 %copy-start.2 = (bf16[8,128,512]{2,1,0:T(8,128)(2,1)S(1)}, bf16[8,128,512]{2,1,0:T(8,128)(2,1)}, u32[]{:S(2)}) copy-start(bf16[8,128,512]{2,1,0:T(8,128)(2,1)} %v_ref.2) | copy-start | bytes 3145732
  42.8 0.8 copy-start.5
  46.8 37.0 %copy-start.9 = (bf16[4,8,3584]{2,1,0:T(8,128)(2,1)S(1)}, bf16[4,8,3584]{2,1,0:T(8,128)(2,1)}, u32[]{:S(2)}) copy-start(bf16[4,8,3584]{2,1,0:T(8,128)(2,1)} %param.18) | copy-start | bytes 688132
  46.8 37.1 %copy-start.11 = (bf16[448,896]{1,0:T(8,128)(2,1)S(1)}, bf16[448,896]{1,0:T(8,128)(2,1)}, u32[]{:S(2)}) copy-start(bf16[448,896]{1,0:T(8,128)(2,1)} %param.22) | copy-start | bytes 2408452
  67.3 16.9 %copy-start.10 = (bf16[1056,896]{1,0:T(8,128)(2,1)S(1)}, bf16[1056,896]{1,0:T(8,128)(2,1)}, u32[]{:S(2)}) copy-start(bf16[1056,896]{1,0:T(8,128)(2,1)} %param.23) | copy-start | bytes 5677060
  68.0 29.2 %copy-start.13 = (f32[896]{0:T(1024)S(1)}, f32[896]{0:T(1024)}, u32[]{:S(2)}) copy-start(f32[896]{0:T(1024)} %param.24) | copy-start | bytes 10756
  83.9 16.6 %copy-start.12 = (bf16[32,3584]{1,0:T(8,128)(2,1)}, bf16[32,3584]{1,0:T(8,128)(2,1)S(1)}, u32[]{:S(2)}) copy-start(bf16[32,3584]{1,0:T(8,128)(2,1)S(1)} %add_convert_fusion.1) | copy-start | bytes 688132
  100.4 7.8 %copy-start.8 = (s32[8]{0:T(128)S(1)}, s32[8]{0:T(128)}, u32[]{:S(2)}) copy-start(s32[8]{0:T(128)} %len_ref.3) | copy-start | bytes 100
  104.0 4.3 %copy-start.3 = (bf16[8,128,512]{2,1,0:T(8,128)(2,1)S(1)}, bf16[8,128,512]{2,1,0:T(8,128)(2,1)}, u32[]{:S(2)}) copy-start(bf16[8,128,512]{2,1,0:T(8,128)(2,1)} %k_ref.3) | copy-start | bytes 3145732
  104.0 4.3 %copy-start.4 = (bf16[8,128,512]{2,1,0:T(8,128)(2,1)S(1)}, bf16[8,128,512]{2,1,0:T(8,128)(2,1)}, u32[]{:S(2)}) copy-start(bf16[8,128,512]{2,1,0:T(8,128)(2,1)} %v_ref.3) | copy-start | bytes 3145732
  117.3 0.7 copy-start.6

commit v5 on v4

--- a/solution.py
+++ b/solution.py
@@ -106,7 +106,7 @@
     dma = pltpu.SemaphoreType.DMA((n - 1,))
     return pl.pallas_call(
         functools.partial(sum_kernel, n, per),
-        out_shape=jax.ShapeDtypeStruct(x.shape, jnp.float32),
+        out_shape=jax.ShapeDtypeStruct(x.shape, jnp.bfloat16),
         in_specs=[vmem],
         out_specs=vmem,
         scratch_shapes=[
@@ -121,7 +121,7 @@
         compiler_params=pltpu.CompilerParams(
             collective_id=ident, has_side_effects=True, vmem_limit_bytes=16 * 2**20
         ),
-    )(x)
+    )(x.astype(jnp.bfloat16)).astype(jnp.float32)
 
 
 def merge_kernel(

time: 136 us -> 135 us (level)
  local copies, waits for them, and re-layouts: 17 us -> 15.3 us
    reshape x1, local copies, waits for them, and re-layouts: 1.48 us -> 0.02 us  [body(): spoken[:, audio_q:audio_q + audio_kv].reshape(rows, AHK, AHD)]
where the time goes in v5:
time: 135 us; the launch traced here: 134 us
  Pallas kernels  98.7 us (73%)
  local copies, waits for them, and re-layouts  15.3 us (11%)
  matrix products  9.8 us (7%)
  other arithmetic  9.02 us (7%)
    pallas_call x3, Pallas kernels, sum_over(): pl.pallas_call(functools.partial(sum_kernel, n, per), out_shape=jax.Shape...  46.7 us
    pallas_call x2, Pallas kernels, merge_over(): pl.pallas_call(functools.partial(merge_kernel, n, per), out_shape=jax.Sha...  33.8 us
    pallas_call x2, Pallas kernels, attend(): pl.pallas_call(functools.partial(attend_kernel, steps, group), grid=(batc...  18.1 us
    dot_general x1, matrix products, body(): spoken = jnp.dot(normed, talker_qkv, preferred_element_type=jnp.float32)  3.22 us
    dot_general x1, matrix products, body(): jnp.dot(mine, thinker_qkv, preferred_element_type=jnp.float32)  3.06 us
    slice x4, local copies, waits for them, and re-layouts, by_row(): x[:, :, :used].reshape(batch, heads, steps, group, -1)  2.86 us

profile of v5, /device:TPU:0, one launch (start us, length us, event | category | flops | bytes accessed | tf_op | source)
XLA Modules:
  0.0 133.9 jit_solution(11848127909114836573)
XLA Ops:
  0.7 0.9 eq.15
  1.6 0.8 dynamic-slice
  3.9 1.1 fusion.3
  5.1 0.8 multiply_cosine_fusion
  5.9 1.0 convert_bitcast_fusion
  6.9 3.1 %convolution_convert_fusion.x_ref = bf16[32,4608]{1,0:T(8,128)(2,1)S(1)} fusion(bf16[448,4608]{1,0:T(8,128)(2,1)} %param.20, f32[32,3584]{1,0:T(8,128)S(1)} %convert_bitcast_fusion, s32[]{:T(128)S(6)} %select_n.4, f32[448]{0:T(512)S(1)} %dynamic-slice), kind=kOutput, calls=%fused_computation | convolution fusion | flops 132296704 | bytes 4491268 | tf_op jit(solution)/shard_map/dot_general | solution.py:328
  9.9 18.5 %shard_map.185 = bf16[32,4608]{1,0:T(8,128)(2,1)S(1)} custom-call(bf16[32,4608]{1,0:T(8,128)(2,1)S(1)} %convolution_convert_fusion.x_ref), custom_call_target="tpu_custom_call" | custom-call | tf_op jit(solution)/shard_map/pallas_call | solution.py:107
  28.6 0.8 slice.78
  29.4 1.9 %reshape.224 = f32[32,28,128]{2,1,0:T(8,128)} reshape(f32[32,3584]{1,0:T(8,128)} %slice.78) | data formatting | bytes 917504 | tf_op jit(solution)/shard_map/reshape | solution.py:331
  31.3 1.6 %subtract_convert_fusion = (bf16[32,28,64]{2,1,0:T(8,128)(2,1)S(1)}, bf16[32,28,64]{2,1,0:T(8,128)(2,1)S(1)}) fusion(f32[32,28,128]{2,1,0:T(8,128)} %reshape.224, f32[32,64]{1,0:T(8,128)S(1)} %get-tuple-element.26, f32[32,64]{1,0:T(8,128)S(1)} %get-tuple-element.27), kind=kLoop, calls=%fused_computation.11 | loop fusion | flops 458752 | bytes 704512 | tf_op jit(solution)/shard_map/convert.18
  33.8 9.1 %shard_map.186 = (bf16[8,4,32,128]{3,2,1,0:T(8,128)(2,1)S(1)}, f32[8,4,32,128]{3,2,1,0:T(8,128)S(1)}) custom-call(s32[8]{0:T(128)S(1)} %copy-done.7, bf16[8,4,32,128]{3,2,1,0:T(8,128)(2,1)S(1)} %pad.29.q_ref, bf16[8,128,512]{2,1,0:T(8,128)(2,1)S(1)} %copy-done.1, bf16[8,128,512]{2,1,0:T(8,128)(2,1)S(1)} %copy-done.2, ...), custom_call_target="tpu_custom_call" | custom-call | tf_op jit(solution)/shard_map/pallas_call | solution.py:261
  42.9 0.8 copy-done.5
  43.9 1.3 copy.35
  46.0 0.9 reshape.241
  47.0 20.4 %shard_map.187 = bf16[32,3584]{1,0:T(8,128)(2,1)S(1)} custom-call(bf16[32,3584]{1,0:T(8,128)(2,1)S(1)} %bitcast.74, f32[32,128]{1,0:T(8,128)S(1)} %pad.32.lse_ref), custom_call_target="tpu_custom_call" | custom-call | tf_op jit(solution)/shard_map/pallas_call | solution.py:184
  68.1 15.8 %shard_map.188 = bf16[32,3584]{1,0:T(8,128)(2,1)S(1)} custom-call(bf16[32,3584]{1,0:T(8,128)(2,1)S(1)} %convolution_convert_fusion.1.x_ref), custom_call_target="tpu_custom_call" | custom-call | tf_op jit(solution)/shard_map/pallas_call | solution.py:107
  85.1 12.4 %shard_map.189 = bf16[32,896]{1,0:T(8,128)(2,1)S(1)} custom-call(bf16[32,896]{1,0:T(8,128)(2,1)S(1)} %fusion.x_ref), custom_call_target="tpu_custom_call" | custom-call | tf_op jit(solution)/shard_map/pallas_call | solution.py:107
  98.3 3.2 %fusion.9 = f32[32,2560]{1,0:T(8,128)S(1)} fusion(bf16[896,2560]{1,0:T(8,128)(2,1)} %param.25, f32[896]{0:T(1024)S(1)} %copy-done.13, f32[32]{0:T(128)S(1)} %add_rsqrt_fusion.1, bf16[32,896]{1,0:T(8,128)(2,1)S(1)} %shard_map.189), kind=kOutput, calls=%fused_computation.32 | convolution fusion | flops 146915328 | bytes 4976256 | tf_op jit(solution)/shard_map/dot_general | solution.py:364
  102.9 1.0 reshape.232
  103.9 1.0 subtract_convert_fusion.1
  107.1 9.0 %shard_map.190 = (bf16[8,4,16,128]{3,2,1,0:T(8,128)(2,1)S(1)}, f32[8,4,16,128]{3,2,1,0:T(8,128)S(1)}) custom-call(s32[8]{0:T(128)S(1)} %copy-done.8, bf16[8,4,16,128]{3,2,1,0:T(8,128)(2,1)S(1)} %pad.33.q_ref, bf16[8,128,512]{2,1,0:T(8,128)(2,1)S(1)} %copy-done.3, bf16[8,128,512]{2,1,0:T(8,128)(2,1)S(1)} %copy-done.4, ...), custom_call_target="tpu_custom_call" | custom-call | tf_op jit(solution)/shard_map/pallas_call | solution.py:261
  116.9 1.3 copy.49
  118.4 13.5 %shard_map.191 = bf16[32,1536]{1,0:T(8,128)(2,1)S(1)} custom-call(bf16[32,1536]{1,0:T(8,128)(2,1)S(1)} %bitcast.76, f32[32,128]{1,0:T(8,128)S(1)} %pad.36.lse_ref), custom_call_target="tpu_custom_call" | custom-call | tf_op jit(solution)/shard_map/pallas_call | solution.py:184
  131.8 2.1 %fusion.2 = bf16[4,8,112]{2,1,0:T(8,128)(2,1)} fusion(bf16[32,1536]{1,0:T(8,128)(2,1)S(1)} %shard_map.191, bf16[1536,896]{1,0:T(8,128)(2,1)} %param.26, s32[]{:T(128)S(6)} %select_n.10, f32[32,896]{1,0:T(8,128)} %convert_element_type.126), kind=kOutput, calls=%fused_computation.6 | convolution fusion | flops 11017216 | bytes 516096 | tf_op jit(solution)/shard_map/dot_general | solution.py:381
  (89 shorter events, 10.6 us)
Async XLA Ops:
  0.6 66.7 %copy-start = (bf16[448,3584]{1,0:T(8,128)(2,1)S(1)}, bf16[448,3584]{1,0:T(8,128)(2,1)}, u32[]{:S(2)}) copy-start(bf16[448,3584]{1,0:T(8,128)(2,1)} %param.21) | copy-start | bytes 9633796
  29.4 4.3 %copy-start.7 = (s32[8]{0:T(128)S(1)}, s32[8]{0:T(128)}, u32[]{:S(2)}) copy-start(s32[8]{0:T(128)} %len_ref.2) | copy-start | bytes 100
  31.3 2.4 %copy-start.1 = (bf16[8,128,512]{2,1,0:T(8,128)(2,1)S(1)}, bf16[8,128,512]{2,1,0:T(8,128)(2,1)}, u32[]{:S(2)}) copy-start(bf16[8,128,512]{2,1,0:T(8,128)(2,1)} %k_ref.2) | copy-start | bytes 3145732
  31.3 2.4 %copy-start.2 = (bf16[8,128,512]{2,1,0:T(8,128)(2,1)S(1)}, bf16[8,128,512]{2,1,0:T(8,128)(2,1)}, u32[]{:S(2)}) copy-start(bf16[8,128,512]{2,1,0:T(8,128)(2,1)} %v_ref.2) | copy-start | bytes 3145732
  42.9 0.8 copy-start.5
  46.9 37.0 %copy-start.9 = (bf16[4,8,3584]{2,1,0:T(8,128)(2,1)S(1)}, bf16[4,8,3584]{2,1,0:T(8,128)(2,1)}, u32[]{:S(2)}) copy-start(bf16[4,8,3584]{2,1,0:T(8,128)(2,1)} %param.18) | copy-start | bytes 688132
  46.9 37.1 %copy-start.11 = (bf16[448,896]{1,0:T(8,128)(2,1)S(1)}, bf16[448,896]{1,0:T(8,128)(2,1)}, u32[]{:S(2)}) copy-start(bf16[448,896]{1,0:T(8,128)(2,1)} %param.22) | copy-start | bytes 2408452
  46.9 37.7 %copy-start.10 = (bf16[1056,896]{1,0:T(8,128)(2,1)S(1)}, bf16[1056,896]{1,0:T(8,128)(2,1)}, u32[]{:S(2)}) copy-start(bf16[1056,896]{1,0:T(8,128)(2,1)} %param.23) | copy-start | bytes 5677060
  67.3 31.0 %copy-start.13 = (f32[896]{0:T(1024)S(1)}, f32[896]{0:T(1024)}, u32[]{:S(2)}) copy-start(f32[896]{0:T(1024)} %param.24) | copy-start | bytes 10756
  84.0 0.7 copy-start.12
  101.5 5.5 %copy-start.8 = (s32[8]{0:T(128)S(1)}, s32[8]{0:T(128)}, u32[]{:S(2)}) copy-start(s32[8]{0:T(128)} %len_ref.3) | copy-start | bytes 100
  103.9 3.2 %copy-start.3 = (bf16[8,128,512]{2,1,0:T(8,128)(2,1)S(1)}, bf16[8,128,512]{2,1,0:T(8,128)(2,1)}, u32[]{:S(2)}) copy-start(bf16[8,128,512]{2,1,0:T(8,128)(2,1)} %k_ref.3) | copy-start | bytes 3145732
  103.9 3.2 %copy-start.4 = (bf16[8,128,512]{2,1,0:T(8,128)(2,1)S(1)}, bf16[8,128,512]{2,1,0:T(8,128)(2,1)}, u32[]{:S(2)}) copy-start(bf16[8,128,512]{2,1,0:T(8,128)(2,1)} %v_ref.3) | copy-start | bytes 3145732
  116.1 0.7 copy-start.6
